TPU v7x, 512 devices: a whole 4x8x8 slice. The times are simulated.
512 devices in a mesh: dp: 32 (over z, x), expert: 16 (over y, core).
Axes of the slice: x: 4, y: 8, z: 8, core: 2. Of those that a mesh axis runs over, the one named last changes fastest.
Arguments:
- tokens: bfloat16 [131072, 1024], P(('dp', 'expert')), may hold values from -6 to 6
- grad_out: bfloat16 [131072, 1024], P(('dp', 'expert')), may hold values from -6 to 6
- combine: bfloat16 [131072, 8], P(('dp', 'expert')), may hold values from 0.049804688 to 1
- expert_ids: int32 [131072, 8], P(('dp', 'expert')), may hold values from 0 to 127, as said below
- slots: int32 [131072, 8], P(('dp', 'expert')), may hold values from -1 to 31, as said below
- w_gate: bfloat16 [16, 1024, 384], P('expert'), may hold values from -0.1875 to 0.1875
- w_up: bfloat16 [16, 1024, 384], P('expert'), may hold values from -0.1875 to 0.1875
- w_down: bfloat16 [16, 384, 1024], P('expert'), may hold values from -0.3125 to 0.3125
Outputs:
- grad_tokens: bfloat16 [131072, 1024], P(('dp', 'expert'))
- grad_combine: bfloat16 [131072, 8], P(('dp', 'expert'))
- grad_w_gate: float32 [16, 1024, 384], P('expert', 'dp')
- grad_w_up: float32 [16, 1024, 384], P('expert', 'dp')
- grad_w_down: float32 [16, 384, 1024], P('expert', None, 'dp')
Inputs may be any that keep to these rules, and one draw needn't show every extreme that they name: `expert_ids`: each row names 8 different experts; experts numbered 16 or above are not computed here. `slots`: a choice of an expert below 16 has as slot the number of earlier rows of the same device (block of 256 rows) that chose the same expert, if that number is below 32; every other choice has -1. In every group of 16 consecutive devices' rows, some expert has 32 active choices from every device of the group.
All inputs are finite; a program needn't handle non-finite values.
Results may differ from a plain program's by a relative error of at most 0.02.
Values may be sent and summed in bfloat16 or wider, within the bound.
No kernel may reach another device: no remote copies, remote signals or barrier semaphores. Data moves between devices by JAX's collectives and lax.ppermute only.
A program may use at most 64 MiB of HBM per device.

v0:
```python
import jax
import jax.numpy as jnp
from jax import lax
from jax.sharding import PartitionSpec as P


def silu_slope(values):
    sig = jax.nn.sigmoid(values)
    return sig * (1.0 + values * (1.0 - sig))


def shards(tokens, grad_out, combine, expert_ids, slots, w_gate, w_up, w_down):
    tok_rows, width = tokens.shape
    local_experts = w_gate.shape[0]
    hidden_units = w_gate.shape[2]
    peers = lax.axis_size("expert")
    capacity = tok_rows // 8
    buffer_rows = local_experts * peers * capacity
    zero_half = jnp.zeros((), jnp.bfloat16)
    position = jnp.where(slots >= 0, expert_ids * capacity + slots, -1)
    matches = position[:, :, None] == jnp.arange(buffer_rows, dtype=jnp.int32)[None, None, :]
    select = jnp.sum(matches.astype(jnp.bfloat16), axis=1)
    contract = (((0,), (0,)), ((), ()))
    sent_x = lax.dot_general(select, tokens, contract, preferred_element_type=jnp.float32).astype(
        jnp.bfloat16
    )
    sent_g = lax.dot_general(select, grad_out, contract, preferred_element_type=jnp.float32).astype(
        jnp.bfloat16
    )
    sent_c = jnp.sum(
        jnp.where(matches, combine.astype(jnp.float32)[:, :, None], 0.0), axis=(0, 1)
    ).astype(jnp.bfloat16)
    got_x, got_g, got_c = (
        lax.all_to_all(sent_x, "expert", split_axis=0, concat_axis=0, tiled=True),
        lax.all_to_all(sent_g, "expert", split_axis=0, concat_axis=0, tiled=True),
        lax.all_to_all(sent_c, "expert", split_axis=0, concat_axis=0, tiled=True),
    )

    def regroup(values):
        shaped = values.reshape((peers, local_experts, capacity) + values.shape[1:])
        return jnp.swapaxes(shaped, 0, 1).reshape(
            (local_experts, peers * capacity) + values.shape[1:]
        )

    def ungroup(values):
        shaped = values.reshape((local_experts, peers, capacity) + values.shape[2:])
        return jnp.swapaxes(shaped, 0, 1).reshape((buffer_rows,) + values.shape[2:])

    buffer_x = regroup(got_x)
    buffer_g = regroup(got_g)
    buffer_c = regroup(got_c)
    gate_pre = jnp.einsum("erd,edf->erf", buffer_x, w_gate, preferred_element_type=jnp.float32)
    up_pre = jnp.einsum("erd,edf->erf", buffer_x, w_up, preferred_element_type=jnp.float32)
    gate_act = jax.nn.silu(gate_pre)
    hidden = (gate_act * up_pre).astype(jnp.bfloat16)
    output = jnp.einsum("erf,efd->erd", hidden, w_down, preferred_element_type=jnp.float32)
    row_combine = jnp.sum(buffer_g.astype(jnp.float32) * output, axis=-1).astype(jnp.bfloat16)
    grad_row = (buffer_c.astype(jnp.float32)[..., None] * buffer_g.astype(jnp.float32)).astype(
        jnp.bfloat16
    )
    grad_hidden = jnp.einsum("erd,efd->erf", grad_row, w_down, preferred_element_type=jnp.float32)
    grad_gate = (grad_hidden * up_pre * silu_slope(gate_pre)).astype(jnp.bfloat16)
    grad_up = (grad_hidden * gate_act).astype(jnp.bfloat16)
    row_input = jnp.einsum("erf,edf->erd", grad_gate, w_gate, preferred_element_type=jnp.float32)
    row_input = (
        row_input + jnp.einsum("erf,edf->erd", grad_up, w_up, preferred_element_type=jnp.float32)
    ).astype(jnp.bfloat16)
    back_x, back_c = (
        lax.all_to_all(ungroup(row_input), "expert", split_axis=0, concat_axis=0, tiled=True),
        lax.all_to_all(ungroup(row_combine), "expert", split_axis=0, concat_axis=0, tiled=True),
    )
    grad_tokens = jnp.dot(select, back_x, preferred_element_type=jnp.float32).astype(jnp.bfloat16)
    grad_combine = jnp.sum(jnp.where(matches, back_c[None, None, :], zero_half), axis=2)
    term_gate = jnp.einsum("erd,erf->def", buffer_x, grad_gate, preferred_element_type=jnp.float32)
    term_up = jnp.einsum("erd,erf->def", buffer_x, grad_up, preferred_element_type=jnp.float32)
    summed = lax.psum_scatter(
        jnp.concatenate([term_gate, term_up], axis=-1).astype(jnp.bfloat16),
        "dp",
        scatter_dimension=0,
        tiled=True,
    ).astype(jnp.float32)
    grad_w_gate = jnp.transpose(summed[:, :, :hidden_units], (1, 0, 2))
    grad_w_up = jnp.transpose(summed[:, :, hidden_units:], (1, 0, 2))
    down_term = jnp.einsum("erf,erd->efd", hidden, grad_row, preferred_element_type=jnp.float32)
    grad_w_down = lax.psum_scatter(
        down_term.astype(jnp.bfloat16), "dp", scatter_dimension=2, tiled=True
    ).astype(jnp.float32)
    return (grad_tokens, grad_combine, grad_w_gate, grad_w_up, grad_w_down)


def solution(mesh):
    placed = (
        P(("dp", "expert"), None),
        P(("dp", "expert"), None),
        P(("dp", "expert"), None),
        P(("dp", "expert"), None),
        P(("dp", "expert"), None),
        P("expert", None, None),
        P("expert", None, None),
        P("expert", None, None),
    )
    return jax.shard_map(
        shards,
        mesh=mesh,
        in_specs=placed,
        out_specs=(
            P(("dp", "expert"), None),
            P(("dp", "expert"), None),
            P("expert", "dp", None),
            P("expert", "dp", None),
            P("expert", None, "dp"),
        ),
        check_vma=False,
    )
```

profile of v0, /device:TPU:1, one launch (start us, length us, event | category | flops | bytes accessed | tf_op | source)
XLA Modules:
  0.0 314.8 jit_solution(5723547381181926149)
XLA Ops:
  7.2 0.0 copy-start
  7.2 0.8 add_select_fusion
  8.0 0.1 copy.32
  8.1 0.8 copy.33
  8.9 0.7 select_reduce_fusion
  9.6 0.7 convert_element_type.181
  10.3 10.1 %all-to-all-start = ((bf16[16,32,1]{1,2,0:T(2,128)(2,1)}), bf16[16,32,1]{1,2,0:T(2,128)(2,1)S(1)}, u32[]{:S(2)}, u32[]{:S(2)}) async-start(bf16[16,32,1]{1,2,0:T(2,128)(2,1)} %convert_element_type.181), calls=%async_computation | async-start | bytes 16384 | tf_op jit(solution)/shard_map/all_to_all | solution.py:36
  20.4 0.0 copy-start.8
  20.4 1.7 fusion.2
  22.1 2.5 convolution_convert_fusion
  24.6 2.8 all-to-all-done
  27.4 4.5 %all-to-all-start.2 = ((bf16[16,32,1024]{2,1,0:T(8,128)(2,1)}), bf16[16,32,1024]{2,1,0:T(8,128)(2,1)S(1)}, u32[]{:S(2)}, u32[]{:S(2)}) async-start(bf16[16,32,1024]{2,1,0:T(8,128)(2,1)} %bitcast.4), calls=%async_computation.2 | async-start | bytes 2097152 | tf_op jit(solution)/shard_map/all_to_all | solution.py:34
  31.9 0.0 copy-done.8
  31.9 1.5 convolution_convert_fusion.1
  33.4 26.4 %all-to-all-done.2 = bf16[16,32,1024]{2,1,0:T(8,128)(2,1)S(1)} async-done(((bf16[16,32,1024]{2,1,0:T(8,128)(2,1)}), bf16[16,32,1024]{2,1,0:T(8,128)(2,1)S(1)}, u32[]{:S(2)}, u32[]{:S(2)}) %all-to-all-start.2) | async-done | bytes 1048608 | tf_op jit(solution)/shard_map/all_to_all | solution.py:34
  59.8 3.6 %all-to-all-start.1 = ((bf16[16,32,1024]{2,1,0:T(8,128)(2,1)}), bf16[16,32,1024]{2,1,0:T(8,128)(2,1)S(1)}, u32[]{:S(2)}, u32[]{:S(2)}) async-start(bf16[16,32,1024]{2,1,0:T(8,128)(2,1)} %bitcast), calls=%async_computation.1 | async-start | bytes 2097152 | tf_op jit(solution)/shard_map/all_to_all | solution.py:35
  63.4 0.1 reshape.220
  63.5 2.7 fusion.15
  66.2 25.1 %all-to-all-done.1 = bf16[16,32,1024]{2,1,0:T(8,128)(2,1)S(1)} async-done(((bf16[16,32,1024]{2,1,0:T(8,128)(2,1)}), bf16[16,32,1024]{2,1,0:T(8,128)(2,1)S(1)}, u32[]{:S(2)}, u32[]{:S(2)}) %all-to-all-start.1) | async-done | bytes 1048608 | tf_op jit(solution)/shard_map/all_to_all | solution.py:35
  91.3 2.3 fusion.10
  93.6 0.0 copy-done.3
  93.6 0.0 copy-done
  93.6 0.0 copy-done.7
  93.6 0.0 copy-start.5
  93.6 1.7 multiply_convert_fusion.1
  95.3 0.0 copy-done.1
  95.3 0.0 copy-done.5
  95.3 0.0 copy-start.2
  95.3 0.0 copy-start.9
  95.3 0.7 fusion.13
  96.1 0.6 copy-done.4
  96.7 1.5 fusion.6
  98.2 0.0 copy-done.10
  98.2 0.0 copy-done.2
  98.2 0.0 copy-done.9
  98.2 0.8 fusion.4
  99.0 0.7 convert_element_type.182
  99.7 3.5 %all-to-all-start.4 = ((bf16[16,32,1]{1,2,0:T(2,128)(2,1)}), bf16[16,32,1]{1,2,0:T(2,128)(2,1)S(1)}, u32[]{:S(2)}, u32[]{:S(2)}) async-start(bf16[16,32,1]{1,2,0:T(2,128)(2,1)} %convert_element_type.182), calls=%async_computation.4 | async-start | bytes 16384 | tf_op jit(solution)/shard_map/all_to_all | solution.py:70
  103.2 0.0 all-reduce.5.cloned.1.call-start
  103.2 0.0 copy-start.6
  103.3 2.0 fusion.7
  105.3 0.0 copy-done.6
  105.3 1.3 pad_maximum_fusion
  106.6 8.4 %copy.36 = bf16[1024,1,768]{2,1,0:T(2,128)(2,1)} copy(bf16[1024,1,768]{0,2,1:T(8,128)(2,1)} %pad_maximum_fusion) | data formatting | bytes 3145728 | tf_op jit(solution)/shard_map/concatenate | solution.py:77
  115.0 1.5 fusion.5
  116.5 0.0 copy-done.11
  116.5 1.5 fusion.8
  118.0 4.8 %copy.37 = bf16[1,384,1024]{1,0,2:T(2,128)(2,1)} copy(bf16[1,384,1024]{2,1,0:T(8,128)(2,1)} %fusion.8) | data formatting | bytes 1572864 | tf_op jit(solution)/shard_map/convert_element_type | solution.py:86
  122.9 0.0 all-reduce.5.cloned.1.call-update
  122.9 2.7 add_convert_fusion
  125.6 0.0 all-to-all-done.4
  125.6 7.2 %all-to-all-start.3 = ((bf16[16,32,1024]{2,1,0:T(8,128)(2,1)}), bf16[16,32,1024]{2,1,0:T(8,128)(2,1)S(1)}, u32[]{:S(2)}, u32[]{:S(2)}) async-start(bf16[16,32,1024]{2,1,0:T(8,128)(2,1)} %bitcast.72), calls=%async_computation.3 | async-start | bytes 2097152 | tf_op jit(solution)/shard_map/all_to_all | solution.py:69
  132.8 1.3 dynamic-slice
  134.8 0.1 broadcast_in_dim.38
  134.9 1.0 fusion.3
  135.9 0.7 copy.38
  136.5 24.2 %all-to-all-done.3 = bf16[16,32,1024]{2,1,0:T(8,128)(2,1)S(1)} async-done(((bf16[16,32,1024]{2,1,0:T(8,128)(2,1)}), bf16[16,32,1024]{2,1,0:T(8,128)(2,1)S(1)}, u32[]{:S(2)}, u32[]{:S(2)}) %all-to-all-start.3) | async-done | bytes 1048608 | tf_op jit(solution)/shard_map/all_to_all | solution.py:69
  160.8 1.2 convolution_convert_fusion.5
  162.0 142.2 %all-reduce.5.cloned.1.call-done = (bf16[1024,1,768]{2,1,0:T(2,128)(2,1)}, bf16[1,384,1024]{1,0,2:T(2,128)(2,1)}) async-done(((bf16[1024,1,768]{2,1,0:T(2,128)(2,1)}, bf16[1,384,1024]{1,0,2:T(2,128)(2,1)}), (bf16[1024,1,768]{2,1,0:T(2,128)(2,1)}, bf16[1,384,1024]{1,0,2:T(2,128)(2,1)})) %all-reduce.5.cloned.1.call-update) | async-done | bytes 2359312
  304.2 1.0 dynamic-slice_convert_fusion
  305.2 0.6 copy.39
  305.9 0.6 copy.40
  306.5 0.8 dynamic-slice_convert_fusion.1
  307.3 0.6 copy.41
  (9 shorter events, 0.1 us)
Async XLA Ops:
  7.2 86.4 %copy-start = (bf16[1,1024,384]{2,1,0:T(8,128)(2,1)S(1)}, bf16[1,1024,384]{2,1,0:T(8,128)(2,1)}, u32[]{:S(2)}) copy-start(bf16[1,1024,384]{2,1,0:T(8,128)(2,1)} %param.14) | copy-start | bytes 2359300
  10.3 17.1 %all-to-all-start = ((bf16[16,32,1]{1,2,0:T(2,128)(2,1)}), bf16[16,32,1]{1,2,0:T(2,128)(2,1)S(1)}, u32[]{:S(2)}, u32[]{:S(2)}) async-start(bf16[16,32,1]{1,2,0:T(2,128)(2,1)} %convert_element_type.181), calls=%async_computation | async-start | bytes 16384 | tf_op jit(solution)/shard_map/all_to_all | solution.py:36
  20.4 11.4 %copy-start.8 = (bf16[256,1024]{1,0:T(8,128)(2,1)S(1)}, bf16[256,1024]{1,0:T(8,128)(2,1)}, u32[]{:S(2)}) copy-start(bf16[256,1024]{1,0:T(8,128)(2,1)} %param.9) | copy-start | bytes 1572868
  27.4 32.4 %all-to-all-start.2 = ((bf16[16,32,1024]{2,1,0:T(8,128)(2,1)}), bf16[16,32,1024]{2,1,0:T(8,128)(2,1)S(1)}, u32[]{:S(2)}, u32[]{:S(2)}) async-start(bf16[16,32,1024]{2,1,0:T(8,128)(2,1)} %bitcast.4), calls=%async_computation.2 | async-start | bytes 2097152 | tf_op jit(solution)/shard_map/all_to_all | solution.py:34
  59.8 33.8 %copy-start.3 = (bf16[16,32,1024]{2,1,0:T(8,128)(2,1)}, bf16[16,32,1024]{2,1,0:T(8,128)(2,1)S(1)}, u32[]{:S(2)}) copy-start(bf16[16,32,1024]{2,1,0:T(8,128)(2,1)S(1)} %all-to-all-done.2) | copy-start | bytes 3145732
  59.8 31.5 %all-to-all-start.1 = ((bf16[16,32,1024]{2,1,0:T(8,128)(2,1)}), bf16[16,32,1024]{2,1,0:T(8,128)(2,1)S(1)}, u32[]{:S(2)}, u32[]{:S(2)}) async-start(bf16[16,32,1024]{2,1,0:T(8,128)(2,1)} %bitcast), calls=%async_computation.1 | async-start | bytes 2097152 | tf_op jit(solution)/shard_map/all_to_all | solution.py:35
  91.3 4.0 %copy-start.1 = (bf16[16,32,1024]{2,1,0:T(8,128)(2,1)}, bf16[16,32,1024]{2,1,0:T(8,128)(2,1)S(1)}, u32[]{:S(2)}) copy-start(bf16[16,32,1024]{2,1,0:T(8,128)(2,1)S(1)} %all-to-all-done.1) | copy-start | bytes 3145732
  91.3 2.3 copy-start.7
  93.6 1.7 copy-start.5
  95.3 2.9 copy-start.10
  95.3 1.4 copy-start.4
  95.3 2.9 copy-start.2
  95.3 2.9 copy-start.9
  99.7 25.9 %all-to-all-start.4 = ((bf16[16,32,1]{1,2,0:T(2,128)(2,1)}), bf16[16,32,1]{1,2,0:T(2,128)(2,1)S(1)}, u32[]{:S(2)}, u32[]{:S(2)}) async-start(bf16[16,32,1]{1,2,0:T(2,128)(2,1)} %convert_element_type.182), calls=%async_computation.4 | async-start | bytes 16384 | tf_op jit(solution)/shard_map/all_to_all | solution.py:70
  103.2 201.0 %all-reduce.5.cloned.1.call-start = ((), (), s32[]{:S(2)}) async-start(), calls=%async_computation.5 | async-start | bytes 9437184
  103.2 2.0 copy-start.6
  115.0 1.5 copy-start.11
  125.6 35.2 %all-to-all-start.3 = ((bf16[16,32,1024]{2,1,0:T(8,128)(2,1)}), bf16[16,32,1024]{2,1,0:T(8,128)(2,1)S(1)}, u32[]{:S(2)}, u32[]{:S(2)}) async-start(bf16[16,32,1024]{2,1,0:T(8,128)(2,1)} %bitcast.72), calls=%async_computation.3 | async-start | bytes 2097152 | tf_op jit(solution)/shard_map/all_to_all | solution.py:69
Sparse Core Ops, SparseCore 0:
  123.0 181.1 all-reduce.4
where the time goes:
time: 316 us; the launch traced here: 315 us
  waiting for transfers between devices  221 us (70%)
  starting transfers between devices  29 us (9%)
  matrix products  21.1 us (7%)
  local copies, waits for them, and re-layouts  20.3 us (6%)
  between operations  14.9 us (5%)
  other arithmetic  8.86 us (3%)
    unnamed x2, waiting for transfers between devices  142 us
    all_to_all x1, waiting for transfers between devices, shards(): lax.all_to_all(sent_x, 'expert', split_axis=0, concat_axis=0, tiled=True)  26.4 us
    all_to_all x1, waiting for transfers between devices, shards(): lax.all_to_all(sent_g, 'expert', split_axis=0, concat_axis=0, tiled=True)  25.1 us
    all_to_all x1, waiting for transfers between devices, shards(): lax.all_to_all(ungroup(row_input), 'expert', split_axis=0, concat_axis=0,...  24.2 us
    all_to_all x1, starting transfers between devices, shards(): lax.all_to_all(sent_c, 'expert', split_axis=0, concat_axis=0, tiled=True)  10.1 us
    concatenate x1, local copies, waits for them, and re-layouts, shards(): jnp.concatenate([term_gate, term_up], axis=-1).astype(jnp.bfloat16)  8.43 us
    all_to_all x1, starting transfers between devices, shards(): lax.all_to_all(ungroup(row_input), 'expert', split_axis=0, concat_axis=0,...  7.24 us
  transfers between devices with their start and end apart: 6, of which 5 were waited for; matrix products, arithmetic and copies ran while one was open for 11% of the time, Pallas kernels for 0%

commit v1 on v0

v1 whole, which is shorter than its diff:
```python
import functools

import jax
import jax.numpy as jnp
from jax import lax
from jax.experimental import pallas as pl
from jax.experimental.pallas import tpu as pltpu
from jax.sharding import Mesh, PartitionSpec as P

X_CHIPS = 4
LANES = 128
F32 = jnp.float32
BF16 = jnp.bfloat16
TN = (((0,), (0,)), ((), ()))
NT = (((1,), (1,)), ((), ()))


def dot(a, b, dims=(((1,), (0,)), ((), ()))):
    return lax.dot_general(a, b, dims, preferred_element_type=F32)


def positions(ids, slots, experts, half_rows):
    half = jnp.where(slots >= half_rows, 1, 0)
    row = half * (experts * half_rows) + ids * half_rows + (slots - half * half_rows)
    return jnp.where(slots >= 0, row, -1)


def dispatch_kernel(experts, half_rows, x_ref, g_ref, c_ref, id_ref, slot_ref, out_ref):
    tokens, width = x_ref.shape
    block = experts * half_rows
    pos = positions(id_ref[...], slot_ref[...], experts, half_rows)
    weights = c_ref[...].astype(F32)
    column = lax.broadcasted_iota(jnp.int32, (tokens, 2 * block), 1)
    routed = jnp.zeros((tokens, 2 * block), F32)
    scaled = jnp.zeros((tokens, 2 * block), F32)
    for k in range(pos.shape[1]):
        match = pos[:, k : k + 1] == column
        routed = jnp.where(match, 1.0, routed)
        scaled = jnp.where(match, weights[:, k : k + 1], scaled)
    routed = routed.astype(BF16)
    scaled = scaled.astype(BF16)
    lane = lax.broadcasted_iota(jnp.int32, (tokens, LANES), 1)
    coded = jnp.zeros((block, LANES), F32)
    for h in range(2):
        pick = routed[:, h * block : (h + 1) * block]
        out_ref[:, h * width : (h + 1) * width] = dot(pick, x_ref[...], TN).astype(BF16)
        out_ref[:, (2 + h) * width : (3 + h) * width] = dot(pick, g_ref[...], TN).astype(BF16)
        mine = jnp.where(lane // (LANES // 2) == h, 1.0, 0.0).astype(BF16)
        coded = coded + dot(scaled[:, h * block : (h + 1) * block], mine, TN)
    out_ref[:, 4 * width :] = coded.astype(BF16)


def expert_kernel(chunk, rows_ref, wgu_ref, wd_ref, back_ref, own_ref, next_ref, far_ref, prev_ref, x_all, r_all, act_all, part):
    block = rows_ref.shape[0]
    hidden_units, width = wd_ref.shape
    wgu = wgu_ref[...]
    wd = wd_ref[...]
    lane = lax.broadcasted_iota(jnp.int32, (block, LANES), 1)
    sums = jnp.zeros((block, LANES), F32)
    for h in range(2):
        x = rows_ref[:, h * width : (h + 1) * width]
        g = rows_ref[:, (2 + h) * width : (3 + h) * width]
        at = 4 * width + h * (LANES // 2)
        c = rows_ref[:, at : at + 1].astype(F32)
        pre = dot(x, wgu)
        gate, up = pre[:, :hidden_units], pre[:, hidden_units:]
        sig = 1.0 / (1.0 + jnp.exp(-gate))
        act = gate * sig
        hidden = (act * up).astype(BF16)
        g_hidden = dot(g, wd, NT)
        row_combine = jnp.sum(hidden.astype(F32) * g_hidden, axis=1, keepdims=True)
        sums = jnp.where(lane // (LANES // 2) == h, row_combine, sums)
        grad_hidden = c * g_hidden
        grad_gate = (grad_hidden * up * (sig * (1.0 + gate * (1.0 - sig)))).astype(BF16)
        grad_up = (grad_hidden * act).astype(BF16)
        lo, hi = h * block, (h + 1) * block
        x_all[lo:hi, :] = x
        r_all[lo:hi, :] = (c * g.astype(F32)).astype(BF16)
        act_all[lo:hi, :hidden_units] = grad_gate
        act_all[lo:hi, hidden_units : 2 * hidden_units] = grad_up
        act_all[lo:hi, 2 * hidden_units :] = hidden
        back_ref[:, h * width : (h + 1) * width] = dot(act_all[lo:hi, : 2 * hidden_units], wgu, NT).astype(BF16)
    back_ref[:, 2 * width :] = sums.astype(BF16)
    step = 256
    for d in range(0, width, step):
        upper = dot(x_all[:, d : d + step], act_all[:, : 2 * hidden_units], TN).astype(BF16)
        lower = dot(r_all[:, d : d + step], act_all[:, 2 * hidden_units :], TN).astype(BF16)
        for j in range(0, step, chunk):
            part[(d + j) // chunk, :, : 2 * hidden_units] = upper[j : j + chunk]
            part[(d + j) // chunk, :, 2 * hidden_units :] = lower[j : j + chunk]
    me = lax.axis_index("x")
    for k, ref in enumerate((own_ref, next_ref, far_ref, prev_ref)):
        x_to = lax.rem(me + k, X_CHIPS)
        for z in range(width // chunk // X_CHIPS):
            ref[z * chunk : (z + 1) * chunk, :] = part[z * X_CHIPS + x_to]


def combine_kernel(experts, half_rows, back_ref, id_ref, slot_ref, grad_ref, comb_ref):
    tokens, width = grad_ref.shape
    block = experts * half_rows
    pos = positions(id_ref[...], slot_ref[...], experts, half_rows)
    column = lax.broadcasted_iota(jnp.int32, (tokens, 2 * block), 1)
    coded = jnp.transpose(back_ref[:, 2 * width :].astype(F32))
    sums = jnp.concatenate([coded[0:1, :], coded[LANES // 2 : LANES // 2 + 1, :]], axis=1)
    routed = jnp.zeros((tokens, 2 * block), F32)
    choice = lax.broadcasted_iota(jnp.int32, (tokens, pos.shape[1]), 1)
    comb = jnp.zeros((tokens, pos.shape[1]), F32)
    for k in range(pos.shape[1]):
        match = pos[:, k : k + 1] == column
        routed = jnp.where(match, 1.0, routed)
        value = jnp.sum(jnp.where(match, sums, 0.0), axis=1, keepdims=True)
        comb = jnp.where(choice == k, value, comb)
    comb_ref[...] = comb.astype(BF16)
    routed = routed.astype(BF16)
    grad = dot(routed[:, :block], back_ref[:, :width]) + dot(routed[:, block:], back_ref[:, width : 2 * width])
    grad_ref[...] = grad.astype(BF16)


def total_kernel(q_ref, gate_ref, up_ref, down_ref):
    hidden_units = gate_ref.shape[1]
    total = jnp.sum(q_ref[...].astype(F32), axis=0)
    gate_ref[...] = total[:, :hidden_units]
    up_ref[...] = total[:, hidden_units : 2 * hidden_units]
    down_ref[...] = jnp.transpose(total[:, 2 * hidden_units :])


def call(kernel, out_shape, args, flops=0, scratch=(), limit=24):
    moved = sum(a.size * a.dtype.itemsize for a in (*args, *out_shape))
    return pl.pallas_call(
        kernel,
        out_shape=out_shape,
        in_specs=[pl.BlockSpec(memory_space=pltpu.VMEM)] * len(args),
        out_specs=[pl.BlockSpec(memory_space=pltpu.VMEM)] * len(out_shape),
        scratch_shapes=scratch,
        compiler_params=pltpu.CompilerParams(vmem_limit_bytes=limit << 20),
        cost_estimate=pl.CostEstimate(flops=flops, bytes_accessed=moved, transcendentals=0),
    )(*args)


def shape(*dims, dtype=BF16):
    return jax.ShapeDtypeStruct(dims, dtype)


def shards(tokens, grad_out, combine, expert_ids, slots, w_gate, w_up, w_down):
    tok_rows, width = tokens.shape
    hidden_units = w_gate.shape[2]
    experts = lax.axis_size("expert")
    z_chips = lax.axis_size("z")
    half_rows = tok_rows // 16
    block = experts * half_rows
    chunk = width // (z_chips * X_CHIPS)
    wgu = jnp.concatenate([w_gate[0], w_up[0]], axis=1)
    wd = w_down[0]

    (sent,) = call(
        functools.partial(dispatch_kernel, experts, half_rows),
        [shape(block, 4 * width + LANES)],
        (tokens, grad_out, combine, expert_ids, slots),
        flops=8 * tok_rows * block * width,
    )
    got = lax.all_to_all(sent, "expert", split_axis=0, concat_axis=0, tiled=True)
    cols = 3 * hidden_units
    piece = shape(z_chips * chunk, cols)
    back, own, nxt, far, prv = call(
        functools.partial(expert_kernel, chunk),
        [shape(block, 2 * width + LANES), piece, piece, piece, piece],
        (got, wgu, wd),
        flops=16 * 2 * block * width * hidden_units,
        scratch=[
            pltpu.VMEM((2 * block, width), BF16),
            pltpu.VMEM((2 * block, width), BF16),
            pltpu.VMEM((2 * block, cols), BF16),
            pltpu.VMEM((width // chunk, chunk, cols), BF16),
        ],
        limit=40,
    )
    returned = lax.all_to_all(back, "expert", split_axis=0, concat_axis=0, tiled=True)

    def shift(values, k):
        return lax.ppermute(values, "x", [(i, (i + k) % X_CHIPS) for i in range(X_CHIPS)])

    from_far = shift(far, 2)
    from_prev = shift(nxt, 1)
    from_next = shift(prv, 3)
    summed = own.astype(F32) + from_prev.astype(F32) + from_next.astype(F32) + from_far.astype(F32)
    summed = summed.astype(BF16)
    summed, returned = lax.optimization_barrier((summed, returned))
    pieces = lax.all_to_all(summed, "z", split_axis=0, concat_axis=0, tiled=True)
    grad_tokens, grad_combine = call(
        functools.partial(combine_kernel, experts, half_rows),
        [shape(tok_rows, width), shape(*slots.shape)],
        (returned, expert_ids, slots),
        flops=4 * tok_rows * block * width,
    )
    grad_gate, grad_up, grad_down = call(
        total_kernel,
        [
            shape(chunk, hidden_units, dtype=F32),
            shape(chunk, hidden_units, dtype=F32),
            shape(hidden_units, chunk, dtype=F32),
        ],
        (pieces.reshape(z_chips, chunk, cols),),
    )
    return grad_tokens, grad_combine, grad_gate[None], grad_up[None], grad_down[None]


def solution(mesh):
    groups, experts = mesh.devices.shape
    split = Mesh(mesh.devices.reshape(groups // X_CHIPS, X_CHIPS, experts), ("z", "x", "expert"))
    dp = ("z", "x")
    rows = P((*dp, "expert"), None)
    weight = P("expert", None, None)
    return jax.shard_map(
        shards,
        mesh=split,
        in_specs=(rows,) * 5 + (weight,) * 3,
        out_specs=(rows, rows, P("expert", dp, None), P("expert", dp, None), P("expert", None, dp)),
        check_vma=False,
    )
```

time: 316 us -> 147 us (0.47)
  waiting for transfers between devices: 221 us -> 86.2 us
  matrix products: 21.1 us -> 0 us
  between operations: 14.9 us -> 0.72 us
  Pallas kernels: 0 us -> 10.8 us
  local copies, waits for them, and re-layouts: 20.3 us -> 10.9 us
  other arithmetic: 8.86 us -> 3.52 us
  starting transfers between devices: 29 us -> 32.5 us
    unnamed x2 -> x0, waiting for transfers between devices: 142 us -> none
    ppermute x0 -> x3, waiting for transfers between devices: none -> 23.2 us  [shift(): lax.ppermute(values, 'x', [(i, (i + k) % X_CHIPS) for i in range(X_CHIPS)])]
    dot_general x12 -> x0, matrix products: 21.1 us -> none  [the longest x1 2.72 us: shards(): jnp.einsum('erd,edf->erf', buffer_x, w_gate, preferred_element_type=jnp.f...]
    all_to_all x5 -> x3, waiting for transfers between devices: 78.5 us -> 63 us  [the longest x1 47.9 us: shards(): lax.all_to_all(sent, 'expert', split_axis=0, concat_axis=0, tiled=True)]
    pallas_call x0 -> x4, Pallas kernels: none -> 10.8 us  [call(): pl.pallas_call(kernel, out_shape=out_shape, in_specs=[pl.BlockSpec(memory...]
    ppermute x0 -> x3, starting transfers between devices: none -> 8.43 us  [shift(): lax.ppermute(values, 'x', [(i, (i + k) % X_CHIPS) for i in range(X_CHIPS)])]
    concatenate x1 -> x0, local copies, waits for them, and re-layouts: 8.43 us -> none  [shards(): jnp.concatenate([term_gate, term_up], axis=-1).astype(jnp.bfloat16)]
    convert_element_type x5 -> x0, local copies, waits for them, and re-layouts: 7.1 us -> none  [the longest x1 4.85 us: shards(): down_term.astype(jnp.bfloat16)]
  transfers between devices with their start and end apart: 6 -> 6, of which waited for: 5 -> 4; matrix products, arithmetic and copies ran while one was open for 11% -> 3% of each run, Pallas kernels for 0% -> 2%
where the time goes in v1:
time: 147 us; the launch traced here: 145 us
  waiting for transfers between devices  86.2 us (59%)
  starting transfers between devices  32.5 us (22%)
  local copies, waits for them, and re-layouts  10.9 us (7%)
  Pallas kernels  10.8 us (7%)
  other arithmetic  3.52 us (2%)
    all_to_all x1, waiting for transfers between devices, shards(): lax.all_to_all(sent, 'expert', split_axis=0, concat_axis=0, tiled=True)  47.9 us
    ppermute x3, waiting for transfers between devices, shift(): lax.ppermute(values, 'x', [(i, (i + k) % X_CHIPS) for i in range(X_CHIPS)])  23.2 us
    all_to_all x1, waiting for transfers between devices, shards(): lax.all_to_all(summed, 'z', split_axis=0, concat_axis=0, tiled=True)  15.1 us
    unnamed x23, local copies, waits for them, and re-layouts  10.9 us
    pallas_call x4, Pallas kernels, call(): pl.pallas_call(kernel, out_shape=out_shape, in_specs=[pl.BlockSpec(memory...  10.8 us
    all_to_all x1, starting transfers between devices, shards(): lax.all_to_all(sent, 'expert', split_axis=0, concat_axis=0, tiled=True)  10.5 us
    ppermute x3, starting transfers between devices, shift(): lax.ppermute(values, 'x', [(i, (i + k) % X_CHIPS) for i in range(X_CHIPS)])  8.43 us
    all_to_all x1, starting transfers between devices, shards(): lax.all_to_all(summed, 'z', split_axis=0, concat_axis=0, tiled=True)  8.4 us
  transfers between devices with their start and end apart: 6, of which 4 were waited for; matrix products, arithmetic and copies ran while one was open for 3% of the time, Pallas kernels for 2%

profile of v1, /device:TPU:1, one launch (start us, length us, event | category | flops | bytes accessed | tf_op | source)
XLA Modules:
  0.0 144.7 jit_solution(10131030349688604600)
XLA Ops:
  0.6 0.8 copy.13.c_ref
  1.4 0.8 copy.14.id_ref
  2.3 0.8 copy.15.slot_ref
  3.1 0.0 copy-start.1
  3.1 1.0 copy-done.1
  4.1 0.0 copy-start.2
  4.1 1.0 copy-done.2
  5.2 3.2 %shard_map.119 = bf16[256,4224]{1,0:T(8,128)(2,1)} custom-call(bf16[256,1024]{1,0:T(8,128)(2,1)S(1)} %copy-done.1, bf16[256,1024]{1,0:T(8,128)(2,1)S(1)} %copy-done.2, bf16[256,8]{1,0:T(8,128)(2,1)S(1)} %copy.13.c_ref, s32[256,8]{1,0:T(8,128)S(1)} %copy.14.id_ref, s32[256,8]{1,0:T(8,128)S(1)} %copy.15.slot_ref), custom_call_target="tpu_custom_call" | custom-call | flops 536870912 | bytes 3231744 | tf_op jit(solution)/shard_map/pallas_call | solution.py:129
  8.4 0.0 copy-start.8
  8.4 10.5 %all-to-all-start = ((bf16[16,16,4224]{2,1,0:T(8,128)(2,1)}), bf16[16,16,4224]{2,1,0:T(8,128)(2,1)S(1)}, u32[]{:S(2)}, u32[]{:S(2)}) async-start(bf16[16,16,4224]{2,1,0:T(8,128)(2,1)} %bitcast), calls=%async_computation | async-start | bytes 4325376 | tf_op jit(solution)/shard_map/all_to_all | solution.py:161
  18.9 0.0 copy-done.8
  18.9 2.4 %pad_maximum_fusion.wgu_ref = bf16[1024,768]{1,0:T(8,128)(2,1)} fusion(bf16[1024,384]{1,0:T(8,128)(2,1)S(1)} %bitcast.16, bf16[1024,384]{1,0:T(8,128)(2,1)} %bitcast.17), kind=kLoop, calls=%fused_computation | loop fusion | flops 3145728 | bytes 3145728 | tf_op jit(solution)/shard_map/concatenate | solution.py:152
  21.3 47.9 %all-to-all-done = bf16[16,16,4224]{2,1,0:T(8,128)(2,1)S(1)} async-done(((bf16[16,16,4224]{2,1,0:T(8,128)(2,1)}), bf16[16,16,4224]{2,1,0:T(8,128)(2,1)S(1)}, u32[]{:S(2)}, u32[]{:S(2)}) %all-to-all-start) | async-done | bytes 2162720 | tf_op jit(solution)/shard_map/all_to_all | solution.py:161
  69.3 0.0 copy-start
  69.3 1.4 copy-done
  70.7 0.0 copy-start.3
  70.7 1.1 copy-done.3
  71.8 4.5 %shard_map.120 = (bf16[256,2176]{1,0:T(8,128)(2,1)}, bf16[256,1152]{1,0:T(8,128)(2,1)S(1)}, bf16[256,1152]{1,0:T(8,128)(2,1)S(1)}, bf16[256,1152]{1,0:T(8,128)(2,1)S(1)}, bf16[256,1152]{1,0:T(8,128)(2,1)S(1)}) custom-call(bf16[256,4224]{1,0:T(8,128)(2,1)S(1)} %bitcast.12, bf16[1024,768]{1,0:T(8,128)(2,1)S(1)} %copy-done, bf16[384,1024]{1,0:T(8,128)(2,1)S(1)} %bitcast.14), custom_call_target="tpu_custom_call" | custom-call | flops 3221225472 | bytes 7995392 | tf_op jit(solution)/shard_map/pallas_call | solution.py:129
  76.3 0.0 copy-start.4
  76.3 0.8 copy-done.4
  77.1 0.0 copy-start.6
  77.1 0.8 copy-done.6
  77.9 0.0 copy-start.7
  77.9 0.8 copy-done.7
  78.8 0.0 copy-start.5
  78.8 5.2 %all-to-all-start.1 = ((bf16[16,16,2176]{2,1,0:T(8,128)(2,1)}), bf16[16,16,2176]{2,1,0:T(8,128)(2,1)S(1)}, u32[]{:S(2)}, u32[]{:S(2)}) async-start(bf16[16,16,2176]{2,1,0:T(8,128)(2,1)} %bitcast.5), calls=%async_computation.1 | async-start | bytes 2228224 | tf_op jit(solution)/shard_map/all_to_all | solution.py:177
  83.9 1.9 %collective-permute-start = (bf16[256,1152]{1,0:T(8,128)(2,1)}, bf16[256,1152]{1,0:T(8,128)(2,1)S(1)}, u32[]{:S(2)}, u32[]{:S(2)}) collective-permute-start(bf16[256,1152]{1,0:T(8,128)(2,1)} %copy-done.7), channel_id=1, source_target_pairs={{0,16},{16,32},{32,48},{48,0},{1,17},{17,33},{33,49},{49,1},{2,18}... | collective-permute-start | bytes 1769480 | tf_op jit(solution)/shard_map/ppermute | solution.py:180
  85.9 4.6 %collective-permute-start.1 = (bf16[256,1152]{1,0:T(8,128)(2,1)}, bf16[256,1152]{1,0:T(8,128)(2,1)S(1)}, u32[]{:S(2)}, u32[]{:S(2)}) collective-permute-start(bf16[256,1152]{1,0:T(8,128)(2,1)} %copy-done.6), channel_id=1, source_target_pairs={{0,48},{16,0},{32,16},{48,32},{1,49},{17,1},{33,17},{49,33},{2,50}... | collective-permute-start | bytes 1769480 | tf_op jit(solution)/shard_map/ppermute | solution.py:180
  90.5 0.0 copy-done.5
  90.5 1.9 %collective-permute-start.2 = (bf16[256,1152]{1,0:T(8,128)(2,1)S(1)}, bf16[256,1152]{1,0:T(8,128)(2,1)S(1)}, u32[]{:S(2)}, u32[]{:S(2)}) collective-permute-start(bf16[256,1152]{1,0:T(8,128)(2,1)S(1)} %copy-done.5), channel_id=1, source_target_pairs={{0,32},{16,48},{32,0},{48,16},{1,33},{17,49},{33,1},{49,17},{2,34}... | collective-permute-start | bytes 1769480 | tf_op jit(solution)/shard_map/ppermute | solution.py:180
  92.4 22.4 %collective-permute-done = bf16[256,1152]{1,0:T(8,128)(2,1)S(1)} collective-permute-done((bf16[256,1152]{1,0:T(8,128)(2,1)}, bf16[256,1152]{1,0:T(8,128)(2,1)S(1)}, u32[]{:S(2)}, u32[]{:S(2)}) %collective-permute-start) | collective-permute-done | bytes 589856 | tf_op jit(solution)/shard_map/ppermute | solution.py:180
  114.8 0.8 collective-permute-done.1
  115.6 0.0 collective-permute-done.2
  115.6 1.1 add_convert_fusion
  116.7 0.0 all-to-all-done.1
  116.7 8.4 %all-to-all-start.2 = ((bf16[8,32,1152]{2,1,0:T(8,128)(2,1)}), bf16[8,32,1152]{2,1,0:T(8,128)(2,1)S(1)}, u32[]{:S(2)}, u32[]{:S(2)}) async-start(bf16[8,32,1152]{2,1,0:T(8,128)(2,1)} %bitcast.15), calls=%async_computation.2 | async-start | bytes 1179648 | tf_op jit(solution)/shard_map/all_to_all | solution.py:188
  125.1 2.3 %shard_map.121 = (bf16[256,1024]{1,0:T(8,128)(2,1)}, bf16[256,8]{1,0:T(8,128)(2,1)S(1)}) custom-call(bf16[256,2176]{1,0:T(8,128)(2,1)S(1)} %bitcast.11, s32[256,8]{1,0:T(8,128)S(1)} %copy.14.id_ref, s32[256,8]{1,0:T(8,128)S(1)} %copy.15.slot_ref), custom_call_target="tpu_custom_call" | custom-call | flops 268435456 | bytes 1658880 | tf_op jit(solution)/shard_map/pallas_call | solution.py:129
  127.5 0.7 copy.18
  128.1 15.1 %all-to-all-done.2.q_ref = bf16[8,32,1152]{2,1,0:T(8,128)(2,1)S(1)} async-done(((bf16[8,32,1152]{2,1,0:T(8,128)(2,1)}), bf16[8,32,1152]{2,1,0:T(8,128)(2,1)S(1)}, u32[]{:S(2)}, u32[]{:S(2)}) %all-to-all-start.2) | async-done | bytes 589856 | tf_op jit(solution)/shard_map/all_to_all | solution.py:188
  143.2 0.7 shard_map.122
  144.0 0.7 copy.19
Async XLA Ops:
  3.1 1.0 copy-start.1
  4.1 1.0 copy-start.2
  8.4 10.5 %copy-start.8 = (bf16[1,1024,384]{2,1,0:T(8,128)(2,1)S(1)}, bf16[1,1024,384]{2,1,0:T(8,128)(2,1)}, u32[]{:S(2)}) copy-start(bf16[1,1024,384]{2,1,0:T(8,128)(2,1)} %param.14) | copy-start | bytes 2359300
  8.4 60.8 %all-to-all-start = ((bf16[16,16,4224]{2,1,0:T(8,128)(2,1)}), bf16[16,16,4224]{2,1,0:T(8,128)(2,1)S(1)}, u32[]{:S(2)}, u32[]{:S(2)}) async-start(bf16[16,16,4224]{2,1,0:T(8,128)(2,1)} %bitcast), calls=%async_computation | async-start | bytes 4325376 | tf_op jit(solution)/shard_map/all_to_all | solution.py:161
  69.3 1.4 copy-start
  70.7 1.1 copy-start.3
  76.3 0.8 copy-start.4
  77.1 0.8 copy-start.6
  77.9 0.8 copy-start.7
  78.8 11.7 %copy-start.5 = (bf16[256,1152]{1,0:T(8,128)(2,1)S(1)}, bf16[256,1152]{1,0:T(8,128)(2,1)}, u32[]{:S(2)}) copy-start(bf16[256,1152]{1,0:T(8,128)(2,1)} %copy-done.4) | copy-start | bytes 1769476
  78.8 38.0 %all-to-all-start.1 = ((bf16[16,16,2176]{2,1,0:T(8,128)(2,1)}), bf16[16,16,2176]{2,1,0:T(8,128)(2,1)S(1)}, u32[]{:S(2)}, u32[]{:S(2)}) async-start(bf16[16,16,2176]{2,1,0:T(8,128)(2,1)} %bitcast.5), calls=%async_computation.1 | async-start | bytes 2228224 | tf_op jit(solution)/shard_map/all_to_all | solution.py:177
  83.9 30.8 %collective-permute-start = (bf16[256,1152]{1,0:T(8,128)(2,1)}, bf16[256,1152]{1,0:T(8,128)(2,1)S(1)}, u32[]{:S(2)}, u32[]{:S(2)}) collective-permute-start(bf16[256,1152]{1,0:T(8,128)(2,1)} %copy-done.7), channel_id=1, source_target_pairs={{0,16},{16,32},{32,48},{48,0},{1,17},{17,33},{33,49},{49,1},{2,18}... | collective-permute-start | bytes 1769480 | tf_op jit(solution)/shard_map/ppermute | solution.py:180
  85.9 29.8 %collective-permute-start.1 = (bf16[256,1152]{1,0:T(8,128)(2,1)}, bf16[256,1152]{1,0:T(8,128)(2,1)S(1)}, u32[]{:S(2)}, u32[]{:S(2)}) collective-permute-start(bf16[256,1152]{1,0:T(8,128)(2,1)} %copy-done.6), channel_id=1, source_target_pairs={{0,48},{16,0},{32,16},{48,32},{1,49},{17,1},{33,17},{49,33},{2,50}... | collective-permute-start | bytes 1769480 | tf_op jit(solution)/shard_map/ppermute | solution.py:180
  90.5 25.1 %collective-permute-start.2 = (bf16[256,1152]{1,0:T(8,128)(2,1)S(1)}, bf16[256,1152]{1,0:T(8,128)(2,1)S(1)}, u32[]{:S(2)}, u32[]{:S(2)}) collective-permute-start(bf16[256,1152]{1,0:T(8,128)(2,1)S(1)} %copy-done.5), channel_id=1, source_target_pairs={{0,32},{16,48},{32,0},{48,16},{1,33},{17,49},{33,1},{49,17},{2,34}... | collective-permute-start | bytes 1769480 | tf_op jit(solution)/shard_map/ppermute | solution.py:180
  116.7 26.5 %all-to-all-start.2 = ((bf16[8,32,1152]{2,1,0:T(8,128)(2,1)}), bf16[8,32,1152]{2,1,0:T(8,128)(2,1)S(1)}, u32[]{:S(2)}, u32[]{:S(2)}) async-start(bf16[8,32,1152]{2,1,0:T(8,128)(2,1)} %bitcast.15), calls=%async_computation.2 | async-start | bytes 1179648 | tf_op jit(solution)/shard_map/all_to_all | solution.py:188

commit v2 on v1

v2 whole, which is shorter than its diff:
```python
import functools

import jax
import jax.numpy as jnp
from jax import lax
from jax.experimental import pallas as pl
from jax.experimental.pallas import tpu as pltpu
from jax.sharding import Mesh, PartitionSpec as P

X_CHIPS = 4
LANES = 128
PACK = 4
CODE = LANES // PACK
FIRST = (0, 2, 1, 3)
F32 = jnp.float32
BF16 = jnp.bfloat16
NN = (((1,), (0,)), ((), ()))
TN = (((0,), (0,)), ((), ()))
NT = (((1,), (1,)), ((), ()))


def dot(a, b, dims=NN):
    return lax.dot_general(a, b, dims, preferred_element_type=F32)


def positions(ids, slots, experts, per):
    group = slots // per
    row = group * (experts * per) + ids * per + (slots - group * per)
    return jnp.where(slots >= 0, row, -1)


def dispatch_kernel(experts, per, x_hbm, g_hbm, c_hbm, id_hbm, slot_hbm, out_hbm,
                    x_ref, g_ref, c_ref, id_ref, slot_ref, out_ref, sems, out_sems):
    tokens, width = x_ref.shape
    block = experts * per
    rows = PACK * block
    fetches = [
        pltpu.make_async_copy(source, ref, sems.at[i])
        for i, (source, ref) in enumerate(
            ((id_hbm, id_ref), (slot_hbm, slot_ref), (c_hbm, c_ref), (x_hbm, x_ref), (g_hbm, g_ref))
        )
    ]
    for fetch in fetches:
        fetch.start()
    fetch_x, fetch_g = fetches[3:]
    for fetch in fetches[:3]:
        fetch.wait()
    pos = positions(id_ref[...], slot_ref[...], experts, per)
    weights = c_ref[...].astype(F32)
    index = lax.broadcasted_iota(jnp.int32, (rows, tokens), 0)
    routed = jnp.zeros((rows, tokens), F32)
    scaled = jnp.zeros((rows, tokens), F32)
    for k in range(pos.shape[0]):
        match = index == pos[k : k + 1, :]
        routed = jnp.where(match, 1.0, routed)
        scaled = jnp.where(match, weights[k : k + 1, :], scaled)
    routed = routed.astype(BF16)
    code = jnp.sum(scaled, axis=1, keepdims=True)
    lane = lax.broadcasted_iota(jnp.int32, (block, LANES), 1)
    coded = jnp.zeros((block, LANES), F32)
    for q in range(PACK):
        coded = jnp.where(lane // CODE == q, code[q * block : (q + 1) * block], coded)
    out_ref[:, 2 * PACK * width :] = coded.astype(BF16)
    fetch_x.wait()
    sent = dot(routed, x_ref[...]).astype(BF16)
    for q in range(PACK):
        out_ref[:, q * width : (q + 1) * width] = sent[q * block : (q + 1) * block]
    half = PACK * width
    first = pltpu.make_async_copy(out_ref.at[:, :half], out_hbm.at[:, :half], out_sems.at[0])
    first.start()
    fetch_g.wait()
    sent = dot(routed, g_ref[...]).astype(BF16)
    for q in range(PACK):
        out_ref[:, half + q * width : half + (q + 1) * width] = sent[q * block : (q + 1) * block]
    second = pltpu.make_async_copy(out_ref.at[:, half:], out_hbm.at[:, half:], out_sems.at[1])
    second.start()
    first.wait()
    second.wait()


def expert_kernel(rows_ref, wg_ref, wu_ref, wd_ref, back_ref, *rest):
    pieces, (x_all, g_all, act_all, part) = rest[:-4], rest[-4:]
    block = back_ref.shape[0]
    hidden_units, width = wd_ref.shape
    rows = PACK * block
    for q in range(PACK):
        x_all[q * block : (q + 1) * block, :] = rows_ref[:, q * width : (q + 1) * width]
        g_all[q * block : (q + 1) * block, :] = rows_ref[:, (PACK + q) * width : (PACK + q + 1) * width]
    lane = lax.broadcasted_iota(jnp.int32, (block, LANES), 1)
    sums = jnp.zeros((block, LANES), F32)
    step = rows // 2
    for lo in range(0, rows, step):
        hi = lo + step
        g = g_all[lo:hi, :]
        c = jnp.concatenate(
            [
                rows_ref[:, 2 * PACK * width + q * CODE : 2 * PACK * width + q * CODE + 1].astype(F32)
                for q in range(lo // block, hi // block)
            ],
            axis=0,
        )
        gate = dot(x_all[lo:hi, :], wg_ref[...])
        up = dot(x_all[lo:hi, :], wu_ref[...])
        sig = 1.0 / (1.0 + jnp.exp(-gate))
        act = gate * sig
        hidden = (act * up).astype(BF16)
        g_hidden = dot(g, wd_ref[...], NT)
        row_combine = jnp.sum(hidden.astype(F32) * g_hidden, axis=1, keepdims=True)
        for q in range(lo // block, hi // block):
            sums = jnp.where(lane // CODE == q, row_combine[q * block - lo : (q + 1) * block - lo], sums)
        grad_hidden = c * g_hidden
        g_all[lo:hi, :] = (c * g.astype(F32)).astype(BF16)
        act_all[lo:hi, :hidden_units] = (grad_hidden * up * (sig * (1.0 + gate * (1.0 - sig)))).astype(BF16)
        act_all[lo:hi, hidden_units : 2 * hidden_units] = (grad_hidden * act).astype(BF16)
        act_all[lo:hi, 2 * hidden_units :] = hidden
    back_ref[:, PACK * width :] = sums.astype(BF16)
    grad = dot(act_all[:, :hidden_units], wg_ref[...], NT)
    grad = (grad + dot(act_all[:, hidden_units : 2 * hidden_units], wu_ref[...], NT)).astype(BF16)
    for q in range(PACK):
        back_ref[:, q * width : (q + 1) * width] = grad[q * block : (q + 1) * block]
    step = 256
    chunk = part.shape[1]
    for d in range(0, width, step):
        upper = dot(x_all[:, d : d + step], act_all[:, : 2 * hidden_units], TN).astype(BF16)
        lower = dot(g_all[:, d : d + step], act_all[:, 2 * hidden_units :], TN).astype(BF16)
        for j in range(0, step, chunk):
            part[(d + j) // chunk, :, : 2 * hidden_units] = upper[j : j + chunk]
            part[(d + j) // chunk, :, 2 * hidden_units :] = lower[j : j + chunk]
    here = lax.axis_index("x")
    for dx, ref in zip(FIRST, pieces, strict=True):
        x_to = lax.rem(here + dx, X_CHIPS)
        for z in range(ref.shape[0]):
            ref[z] = part[z * X_CHIPS + x_to]


def partial_kernel(*refs):
    total = refs[0][...].astype(F32)
    for ref in refs[1:-1]:
        total = total + ref[...].astype(F32)
    refs[-1][...] = total.astype(BF16)


def combine_kernel(experts, per, back_ref, id_ref, slot_ref, grad_ref, comb_ref):
    tokens, width = grad_ref.shape
    block = experts * per
    rows = PACK * block
    pos = positions(id_ref[...], slot_ref[...], experts, per)
    index = lax.broadcasted_iota(jnp.int32, (rows, tokens), 0)
    code = jnp.concatenate(
        [
            back_ref[:, PACK * width + q * CODE : PACK * width + q * CODE + 1].astype(F32)
            for q in range(PACK)
        ],
        axis=0,
    )
    routed = jnp.zeros((rows, tokens), F32)
    choice = lax.broadcasted_iota(jnp.int32, pos.shape, 0)
    comb = jnp.zeros(pos.shape, F32)
    for k in range(pos.shape[0]):
        match = index == pos[k : k + 1, :]
        routed = jnp.where(match, 1.0, routed)
        value = jnp.sum(jnp.where(match, code, 0.0), axis=0, keepdims=True)
        comb = jnp.where(choice == k, value, comb)
    comb_ref[...] = comb.astype(BF16)
    routed = routed.astype(BF16)
    grad = jnp.zeros((tokens, width), F32)
    for q in range(PACK):
        grad = grad + dot(routed[q * block : (q + 1) * block], back_ref[:, q * width : (q + 1) * width], TN)
    grad_ref[...] = grad.astype(BF16)


def total_kernel(parts_ref, gate_ref, up_ref, down_ref):
    hidden_units = gate_ref.shape[1]
    total = jnp.sum(parts_ref[...].astype(F32), axis=0)
    gate_ref[...] = total[:, :hidden_units]
    up_ref[...] = total[:, hidden_units : 2 * hidden_units]
    down_ref[...] = total[:, 2 * hidden_units :]


def call(kernel, out_shape, args, flops=0, scratch=(), limit=24, ins="", outs=""):
    moved = sum(a.size * a.dtype.itemsize for a in (*args, *out_shape))

    def specs(letters, count):
        letters = letters.ljust(count, "v")
        return [pl.BlockSpec(memory_space=pltpu.HBM if c == "h" else pltpu.VMEM) for c in letters]

    return pl.pallas_call(
        kernel,
        out_shape=out_shape,
        in_specs=specs(ins, len(args)),
        out_specs=specs(outs, len(out_shape)),
        scratch_shapes=scratch,
        compiler_params=pltpu.CompilerParams(vmem_limit_bytes=limit << 20),
        cost_estimate=pl.CostEstimate(flops=flops, bytes_accessed=moved, transcendentals=0),
    )(*args)


def shape(*dims, dtype=BF16):
    return jax.ShapeDtypeStruct(dims, dtype)


def shards(tokens, grad_out, combine, expert_ids, slots, w_gate, w_up, w_down):
    tok_rows, width = tokens.shape
    hidden_units = w_gate.shape[2]
    experts = lax.axis_size("expert")
    z_chips = lax.axis_size("z")
    per = tok_rows // 8 // PACK
    block = experts * per
    rows = PACK * block
    chunk = width // (z_chips * X_CHIPS)
    cols = 3 * hidden_units
    ids_t, slots_t, combine_t = expert_ids.T, slots.T, combine.T

    (sent,) = call(
        functools.partial(dispatch_kernel, experts, per),
        [shape(block, 2 * PACK * width + LANES)],
        (tokens, grad_out, combine_t, ids_t, slots_t),
        flops=4 * tok_rows * rows * width,
        scratch=[
            pltpu.VMEM((tok_rows, width), BF16),
            pltpu.VMEM((tok_rows, width), BF16),
            pltpu.VMEM(combine_t.shape, BF16),
            pltpu.VMEM(ids_t.shape, jnp.int32),
            pltpu.VMEM(slots_t.shape, jnp.int32),
            pltpu.VMEM((block, 2 * PACK * width + LANES), BF16),
            pltpu.SemaphoreType.DMA((5,)),
            pltpu.SemaphoreType.DMA((2,)),
        ],
        limit=60,
        ins="hhhhh",
        outs="h",
    )
    got = lax.all_to_all(sent, "expert", split_axis=0, concat_axis=0, tiled=True)
    piece = shape(z_chips, chunk, cols)
    back, own, *pieces = call(
        expert_kernel,
        [shape(block, PACK * width + LANES)] + [piece] * len(FIRST),
        (got, w_gate[0], w_up[0], w_down[0]),
        flops=16 * rows * width * hidden_units,
        scratch=[
            pltpu.VMEM((rows, width), BF16),
            pltpu.VMEM((rows, width), BF16),
            pltpu.VMEM((rows, cols), BF16),
            pltpu.VMEM((width // chunk, chunk, cols), BF16),
        ],
    )

    returned = lax.all_to_all(back, "expert", split_axis=0, concat_axis=0, tiled=True)
    arrived = [
        lax.ppermute(values, "x", [(i, (i + dx) % X_CHIPS) for i in range(X_CHIPS)])
        for values, dx in zip(pieces, FIRST[1:], strict=True)
    ]
    (summed,) = call(partial_kernel, [piece], (own, *arrived), limit=16)
    summed, returned = lax.optimization_barrier((summed, returned))
    parts = lax.all_to_all(summed, "z", split_axis=0, concat_axis=0, tiled=True)
    grad_tokens, grad_combine = call(
        functools.partial(combine_kernel, experts, per),
        [shape(tok_rows, width), shape(*ids_t.shape)],
        (returned, ids_t, slots_t),
        flops=2 * tok_rows * rows * width,
    )
    grads = call(total_kernel, [shape(chunk, hidden_units, dtype=F32)] * 3, (parts,))
    return grad_tokens, grad_combine.T, grads[0][None], grads[1][None], grads[2].T[None]


def solution(mesh):
    groups, experts = mesh.devices.shape
    split = Mesh(mesh.devices.reshape(groups // X_CHIPS, X_CHIPS, experts), ("z", "x", "expert"))
    dp = ("z", "x")
    rows = P((*dp, "expert"), None)
    weight = P("expert", None, None)
    return jax.shard_map(
        shards,
        mesh=split,
        in_specs=(rows,) * 5 + (weight,) * 3,
        out_specs=(rows, rows, P("expert", dp, None), P("expert", dp, None), P("expert", None, dp)),
        check_vma=False,
    )
```

time: 147 us -> 137 us (0.932)
  blocking collectives: 0 us -> 62.7 us
  waiting for transfers between devices: 86.2 us -> 39.3 us
  starting transfers between devices: 32.5 us -> 21.5 us
  local copies, waits for them, and re-layouts: 10.9 us -> 0.03 us
  other arithmetic: 3.52 us -> 0 us
    all_to_all x0 -> x1, blocking collectives: none -> 62.7 us  [shards(): lax.all_to_all(sent, 'expert', split_axis=0, concat_axis=0, tiled=True)]
    all_to_all x2 -> x1, waiting for transfers between devices: 63 us -> 17.4 us  [shards(): parts = lax.all_to_all(summed, 'z', split_axis=0, concat_axis=0, tiled=True)]
    unnamed x23 -> x10, local copies, waits for them, and re-layouts: 10.9 us -> 0.03 us
    all_to_all x2 -> x1, starting transfers between devices: 18.9 us -> 8.23 us  [shards(): parts = lax.all_to_all(summed, 'z', split_axis=0, concat_axis=0, tiled=True)]
    concatenate x1 -> x0, other arithmetic: 2.41 us -> none  [shards(): wgu = jnp.concatenate([w_gate[0], w_up[0]], axis=1)]
    pallas_call x4 -> x5, Pallas kernels: 10.8 us -> 11.9 us  [call(): pl.pallas_call(kernel, out_shape=out_shape, in_specs=specs(ins, len(args)...]
  transfers between devices with their start and end apart: 6 -> 5, of which waited for: 4 -> 3; matrix products, arithmetic and copies ran while one was open for 3% -> 0% of each run, Pallas kernels for 2% -> 2%
where the time goes in v2:
time: 137 us; the launch traced here: 136 us
  blocking collectives  62.7 us (46%)
  waiting for transfers between devices  39.3 us (29%)
  starting transfers between devices  21.5 us (16%)
  Pallas kernels  11.9 us (9%)
    all_to_all x1, blocking collectives, shards(): lax.all_to_all(sent, 'expert', split_axis=0, concat_axis=0, tiled=True)  62.7 us
    ppermute x3, waiting for transfers between devices, shards(): lax.ppermute(values, 'x', [(i, (i + dx) % X_CHIPS) for i in range(X_CHIPS)])  21.9 us
    all_to_all x1, waiting for transfers between devices, shards(): parts = lax.all_to_all(summed, 'z', split_axis=0, concat_axis=0, tiled=True)  17.4 us
    pallas_call x5, Pallas kernels, call(): pl.pallas_call(kernel, out_shape=out_shape, in_specs=specs(ins, len(args)...  11.9 us
    ppermute x3, starting transfers between devices, shards(): lax.ppermute(values, 'x', [(i, (i + dx) % X_CHIPS) for i in range(X_CHIPS)])  9.35 us
    all_to_all x1, starting transfers between devices, shards(): parts = lax.all_to_all(summed, 'z', split_axis=0, concat_axis=0, tiled=True)  8.23 us
    all_to_all x1, starting transfers between devices, shards(): lax.all_to_all(back, 'expert', split_axis=0, concat_axis=0, tiled=True)  3.89 us
  transfers between devices with their start and end apart: 5, of which 3 were waited for; matrix products, arithmetic and copies ran while one was open for 0% of the time, Pallas kernels for 2%

profile of v2, /device:TPU:1, one launch (start us, length us, event | category | flops | bytes accessed | tf_op | source)
XLA Modules:
  0.0 136.1 jit_solution(71280528065650315)
XLA Ops:
  0.6 3.3 %shard_map.119 = bf16[128,8320]{1,0:T(8,128)(2,1)} custom-call(bf16[256,1024]{1,0:T(8,128)(2,1)} %x_hbm.1, bf16[256,1024]{1,0:T(8,128)(2,1)} %g_hbm.1, bf16[8,256]{1,0:T(8,128)(2,1)} %bitcast.26, s32[8,256]{1,0:T(8,128)} %bitcast.18, s32[8,256]{1,0:T(8,128)} %bitcast.20), custom_call_target="tpu_custom_call" | custom-call | flops 536870912 | bytes 3198976 | tf_op jit(solution)/shard_map/pallas_call | solution.py:187
  4.0 0.0 copy-start.2
  4.0 0.0 copy-start.3
  4.0 0.0 copy-start.4
  4.0 62.7 %all_to_all.28 = bf16[16,8,8320]{2,1,0:T(8,128)(2,1)S(1)} all-to-all(bf16[16,8,8320]{2,1,0:T(8,128)(2,1)} %bitcast.25), channel_id=1, replica_groups=mesh['z'=8,'x'=4,'expert'=16] {'expert'}, dimensions={0} | all-to-all | bytes 4259840 | tf_op jit(solution)/shard_map/all_to_all | solution.py:233
  66.7 0.0 copy-done.2
  66.7 0.0 copy-done.3
  66.7 0.0 copy-done.4
  66.7 4.8 %shard_map.120 = (bf16[128,4224]{1,0:T(8,128)(2,1)}, bf16[8,32,1152]{2,1,0:T(8,128)(2,1)S(1)}, bf16[8,32,1152]{2,1,0:T(8,128)(2,1)S(1)}, bf16[8,32,1152]{2,1,0:T(8,128)(2,1)S(1)}, bf16[8,32,1152]{2,1,0:T(8,128)(2,1)S(1)}) custom-call(bf16[128,8320]{1,0:T(8,128)(2,1)S(1)} %bitcast.17, bf16[1024,384]{1,0:T(8,128)(2,1)S(1)} %bitcast.22, ...), custom_call_target="tpu_custom_call" | custom-call | flops 3221225472 | bytes 7929856 | tf_op jit(solution)/shard_map/pallas_call | solution.py:187
  71.4 3.9 %all-to-all-start.1 = ((bf16[16,8,4224]{2,1,0:T(8,128)(2,1)}), bf16[16,8,4224]{2,1,0:T(8,128)(2,1)S(1)}, u32[]{:S(2)}, u32[]{:S(2)}) async-start(bf16[16,8,4224]{2,1,0:T(8,128)(2,1)} %bitcast.8), calls=%async_computation.1 | async-start | bytes 2162688 | tf_op jit(solution)/shard_map/all_to_all | solution.py:248
  75.3 0.0 copy-start
  75.3 0.0 copy-start.1
  75.4 2.9 %collective-permute-start = (bf16[8,32,1152]{2,1,0:T(8,128)(2,1)S(1)}, bf16[8,32,1152]{2,1,0:T(8,128)(2,1)S(1)}, u32[]{:S(2)}, u32[]{:S(2)}) collective-permute-start(bf16[8,32,1152]{2,1,0:T(8,128)(2,1)S(1)} %get-tuple-element.18), channel_id=1, source_target_pairs={{0,32},{16,48},{32,0},{48,16},{1,33},{17,49},{33,1},{49,17},{2,34}... | collective-permute-start | bytes 1769480 | tf_op jit(solution)/shard_map/ppermute | solution.py:250
  78.2 2.2 %collective-permute-start.1 = (bf16[8,32,1152]{2,1,0:T(8,128)(2,1)S(1)}, bf16[8,32,1152]{2,1,0:T(8,128)(2,1)S(1)}, u32[]{:S(2)}, u32[]{:S(2)}) collective-permute-start(bf16[8,32,1152]{2,1,0:T(8,128)(2,1)S(1)} %get-tuple-element.19), channel_id=1, source_target_pairs={{0,16},{16,32},{32,48},{48,0},{1,17},{17,33},{33,49},{49,1},{2,18}... | collective-permute-start | bytes 1769480 | tf_op jit(solution)/shard_map/ppermute | solution.py:250
  80.4 4.3 %collective-permute-start.2 = (bf16[8,32,1152]{2,1,0:T(8,128)(2,1)S(1)}, bf16[8,32,1152]{2,1,0:T(8,128)(2,1)S(1)}, u32[]{:S(2)}, u32[]{:S(2)}) collective-permute-start(bf16[8,32,1152]{2,1,0:T(8,128)(2,1)S(1)} %get-tuple-element.20), channel_id=1, source_target_pairs={{0,48},{16,0},{32,16},{48,32},{1,49},{17,1},{33,17},{49,33},{2,50}... | collective-permute-start | bytes 1769480 | tf_op jit(solution)/shard_map/ppermute | solution.py:250
  84.7 8.8 %collective-permute-done.refs_1_ = bf16[8,32,1152]{2,1,0:T(8,128)(2,1)S(1)} collective-permute-done((bf16[8,32,1152]{2,1,0:T(8,128)(2,1)S(1)}, bf16[8,32,1152]{2,1,0:T(8,128)(2,1)S(1)}, u32[]{:S(2)}, u32[]{:S(2)}) %collective-permute-start) | collective-permute-done | bytes 589856 | tf_op jit(solution)/shard_map/ppermute | solution.py:250
  93.5 13.1 %collective-permute-done.1.refs_2_ = bf16[8,32,1152]{2,1,0:T(8,128)(2,1)S(1)} collective-permute-done((bf16[8,32,1152]{2,1,0:T(8,128)(2,1)S(1)}, bf16[8,32,1152]{2,1,0:T(8,128)(2,1)S(1)}, u32[]{:S(2)}, u32[]{:S(2)}) %collective-permute-start.1) | collective-permute-done | bytes 589856 | tf_op jit(solution)/shard_map/ppermute | solution.py:250
  106.7 0.0 collective-permute-done.2.refs_3_
  106.7 1.1 shard_map.121
  107.8 0.0 all-to-all-done.1
  107.8 8.2 %all-to-all-start.2 = ((bf16[8,32,1152]{2,1,0:T(8,128)(2,1)}), bf16[8,32,1152]{2,1,0:T(8,128)(2,1)S(1)}, u32[]{:S(2)}, u32[]{:S(2)}) async-start(bf16[8,32,1152]{2,1,0:T(8,128)(2,1)} %shard_map.121), calls=%async_computation.2 | async-start | bytes 1179648 | tf_op jit(solution)/shard_map/all_to_all | solution.py:255
  116.0 0.0 copy-done
  116.0 0.0 copy-done.1
  116.0 2.0 %shard_map.122 = (bf16[256,1024]{1,0:T(8,128)(2,1)}, bf16[8,256]{1,0:T(8,128)(2,1)}) custom-call(bf16[128,4224]{1,0:T(8,128)(2,1)S(1)} %bitcast.16, s32[8,256]{1,0:T(8,128)S(1)} %bitcast.19, s32[8,256]{1,0:T(8,128)S(1)} %bitcast.21), custom_call_target="tpu_custom_call" | custom-call | flops 268435456 | bytes 1626112 | tf_op jit(solution)/shard_map/pallas_call | solution.py:187
  118.0 17.4 %all-to-all-done.2.parts_ref = bf16[8,32,1152]{2,1,0:T(8,128)(2,1)S(1)} async-done(((bf16[8,32,1152]{2,1,0:T(8,128)(2,1)}), bf16[8,32,1152]{2,1,0:T(8,128)(2,1)S(1)}, u32[]{:S(2)}, u32[]{:S(2)}) %all-to-all-start.2) | async-done | bytes 589856 | tf_op jit(solution)/shard_map/all_to_all | solution.py:255
  135.4 0.7 shard_map.123
Async XLA Ops:
  4.0 62.7 %copy-start.2 = (bf16[1,1024,384]{2,1,0:T(8,128)(2,1)S(1)}, bf16[1,1024,384]{2,1,0:T(8,128)(2,1)}, u32[]{:S(2)}) copy-start(bf16[1,1024,384]{2,1,0:T(8,128)(2,1)} %param.13) | copy-start | bytes 2359300
  4.0 62.7 %copy-start.3 = (bf16[1,1024,384]{2,1,0:T(8,128)(2,1)S(1)}, bf16[1,1024,384]{2,1,0:T(8,128)(2,1)}, u32[]{:S(2)}) copy-start(bf16[1,1024,384]{2,1,0:T(8,128)(2,1)} %param.14) | copy-start | bytes 2359300
  4.0 62.7 %copy-start.4 = (bf16[1,384,1024]{2,1,0:T(8,128)(2,1)S(1)}, bf16[1,384,1024]{2,1,0:T(8,128)(2,1)}, u32[]{:S(2)}) copy-start(bf16[1,384,1024]{2,1,0:T(8,128)(2,1)} %param.15) | copy-start | bytes 2359300
  71.4 36.3 %all-to-all-start.1 = ((bf16[16,8,4224]{2,1,0:T(8,128)(2,1)}), bf16[16,8,4224]{2,1,0:T(8,128)(2,1)S(1)}, u32[]{:S(2)}, u32[]{:S(2)}) async-start(bf16[16,8,4224]{2,1,0:T(8,128)(2,1)} %bitcast.8), calls=%async_computation.1 | async-start | bytes 2162688 | tf_op jit(solution)/shard_map/all_to_all | solution.py:248
  75.3 40.7 %copy-start = (s32[256,8]{0,1:T(8,128)S(1)}, s32[256,8]{0,1:T(8,128)}, u32[]{:S(2)}) copy-start(s32[256,8]{0,1:T(8,128)} %param.11) | copy-start | bytes 24580
  75.3 40.7 %copy-start.1 = (s32[256,8]{0,1:T(8,128)S(1)}, s32[256,8]{0,1:T(8,128)}, u32[]{:S(2)}) copy-start(s32[256,8]{0,1:T(8,128)} %param.12) | copy-start | bytes 24580
  75.4 18.1 %collective-permute-start = (bf16[8,32,1152]{2,1,0:T(8,128)(2,1)S(1)}, bf16[8,32,1152]{2,1,0:T(8,128)(2,1)S(1)}, u32[]{:S(2)}, u32[]{:S(2)}) collective-permute-start(bf16[8,32,1152]{2,1,0:T(8,128)(2,1)S(1)} %get-tuple-element.18), channel_id=1, source_target_pairs={{0,32},{16,48},{32,0},{48,16},{1,33},{17,49},{33,1},{49,17},{2,34}... | collective-permute-start | bytes 1769480 | tf_op jit(solution)/shard_map/ppermute | solution.py:250
  78.2 28.4 %collective-permute-start.1 = (bf16[8,32,1152]{2,1,0:T(8,128)(2,1)S(1)}, bf16[8,32,1152]{2,1,0:T(8,128)(2,1)S(1)}, u32[]{:S(2)}, u32[]{:S(2)}) collective-permute-start(bf16[8,32,1152]{2,1,0:T(8,128)(2,1)S(1)} %get-tuple-element.19), channel_id=1, source_target_pairs={{0,16},{16,32},{32,48},{48,0},{1,17},{17,33},{33,49},{49,1},{2,18}... | collective-permute-start | bytes 1769480 | tf_op jit(solution)/shard_map/ppermute | solution.py:250
  80.4 26.2 %collective-permute-start.2 = (bf16[8,32,1152]{2,1,0:T(8,128)(2,1)S(1)}, bf16[8,32,1152]{2,1,0:T(8,128)(2,1)S(1)}, u32[]{:S(2)}, u32[]{:S(2)}) collective-permute-start(bf16[8,32,1152]{2,1,0:T(8,128)(2,1)S(1)} %get-tuple-element.20), channel_id=1, source_target_pairs={{0,48},{16,0},{32,16},{48,32},{1,49},{17,1},{33,17},{49,33},{2,50}... | collective-permute-start | bytes 1769480 | tf_op jit(solution)/shard_map/ppermute | solution.py:250
  107.8 27.6 %all-to-all-start.2 = ((bf16[8,32,1152]{2,1,0:T(8,128)(2,1)}), bf16[8,32,1152]{2,1,0:T(8,128)(2,1)S(1)}, u32[]{:S(2)}, u32[]{:S(2)}) async-start(bf16[8,32,1152]{2,1,0:T(8,128)(2,1)} %shard_map.121), calls=%async_computation.2 | async-start | bytes 1179648 | tf_op jit(solution)/shard_map/all_to_all | solution.py:255

commit v3 on v2

--- a/solution.py
+++ b/solution.py
@@ -11,7 +11,8 @@
 LANES = 128
 PACK = 4
 CODE = LANES // PACK
-FIRST = (0, 2, 1, 3)
+LOW = 2
+FIRST = ((0, 0), (2, 1), (2, 0), (0, 1), (1, 0), (3, 0), (1, 1), (3, 1))
 F32 = jnp.float32
 BF16 = jnp.bfloat16
 NN = (((1,), (0,)), ((), ()))
@@ -62,24 +63,22 @@
         coded = jnp.where(lane // CODE == q, code[q * block : (q + 1) * block], coded)
     out_ref[:, 2 * PACK * width :] = coded.astype(BF16)
     fetch_x.wait()
-    sent = dot(routed, x_ref[...]).astype(BF16)
-    for q in range(PACK):
-        out_ref[:, q * width : (q + 1) * width] = sent[q * block : (q + 1) * block]
-    half = PACK * width
-    first = pltpu.make_async_copy(out_ref.at[:, :half], out_hbm.at[:, :half], out_sems.at[0])
-    first.start()
-    fetch_g.wait()
-    sent = dot(routed, g_ref[...]).astype(BF16)
-    for q in range(PACK):
-        out_ref[:, half + q * width : half + (q + 1) * width] = sent[q * block : (q + 1) * block]
-    second = pltpu.make_async_copy(out_ref.at[:, half:], out_hbm.at[:, half:], out_sems.at[1])
-    second.start()
-    first.wait()
-    second.wait()
-
-
-def expert_kernel(rows_ref, wg_ref, wu_ref, wd_ref, back_ref, *rest):
-    pieces, (x_all, g_all, act_all, part) = rest[:-4], rest[-4:]
+    sends = []
+    for i, (fetch, ref) in enumerate(((None, x_ref), (fetch_g, g_ref))):
+        if fetch is not None:
+            fetch.wait()
+        for q in range(PACK):
+            lo = (i * PACK + q) * width
+            hi = lo + width if (i, q) != (1, PACK - 1) else out_ref.shape[1]
+            out_ref[:, lo : lo + width] = dot(routed[q * block : (q + 1) * block], ref[...]).astype(BF16)
+            sends.append(pltpu.make_async_copy(out_ref.at[:, lo:hi], out_hbm.at[:, lo:hi], out_sems.at[len(sends)]))
+            sends[-1].start()
+    for send in sends:
+        send.wait()
+
+
+def expert_kernel(rows_ref, wg_ref, wu_ref, wd_ref, back_hbm, *rest):
+    pieces, (x_all, g_all, act_all, part, back_ref, sem) = rest[:-6], rest[-6:]
     block = back_ref.shape[0]
     hidden_units, width = wd_ref.shape
     rows = PACK * block
@@ -118,19 +117,22 @@
     grad = (grad + dot(act_all[:, hidden_units : 2 * hidden_units], wu_ref[...], NT)).astype(BF16)
     for q in range(PACK):
         back_ref[:, q * width : (q + 1) * width] = grad[q * block : (q + 1) * block]
-    step = 256
-    chunk = part.shape[1]
-    for d in range(0, width, step):
-        upper = dot(x_all[:, d : d + step], act_all[:, : 2 * hidden_units], TN).astype(BF16)
-        lower = dot(g_all[:, d : d + step], act_all[:, 2 * hidden_units :], TN).astype(BF16)
-        for j in range(0, step, chunk):
-            part[(d + j) // chunk, :, : 2 * hidden_units] = upper[j : j + chunk]
-            part[(d + j) // chunk, :, 2 * hidden_units :] = lower[j : j + chunk]
-    here = lax.axis_index("x")
-    for dx, ref in zip(FIRST, pieces, strict=True):
-        x_to = lax.rem(here + dx, X_CHIPS)
-        for z in range(ref.shape[0]):
-            ref[z] = part[z * X_CHIPS + x_to]
+    store = pltpu.make_async_copy(back_ref, back_hbm, sem)
+    store.start()
+    x_here, low_here = lax.axis_index("x"), lax.axis_index("zl")
+    places = [lax.rem(low_here + dz, LOW) * X_CHIPS + lax.rem(x_here + dx, X_CHIPS) for dx, dz in FIRST]
+    chunk = part.shape[2]
+    step = chunk * len(FIRST)
+    for z in range(width // step):
+        lo, hi = z * step, (z + 1) * step
+        upper = dot(x_all[:, lo:hi], act_all[:, : 2 * hidden_units], TN).astype(BF16)
+        lower = dot(g_all[:, lo:hi], act_all[:, 2 * hidden_units :], TN).astype(BF16)
+        for j in range(len(FIRST)):
+            part[z, j, :, : 2 * hidden_units] = upper[j * chunk : (j + 1) * chunk]
+            part[z, j, :, 2 * hidden_units :] = lower[j * chunk : (j + 1) * chunk]
+        for place, ref in zip(places, pieces, strict=True):
+            ref[z] = part[z, place]
+    store.wait()
 
 
 def partial_kernel(*refs):
@@ -203,11 +205,11 @@
     tok_rows, width = tokens.shape
     hidden_units = w_gate.shape[2]
     experts = lax.axis_size("expert")
-    z_chips = lax.axis_size("z")
+    high = lax.axis_size("zh")
     per = tok_rows // 8 // PACK
     block = experts * per
     rows = PACK * block
-    chunk = width // (z_chips * X_CHIPS)
+    chunk = width // (high * LOW * X_CHIPS)
     cols = 3 * hidden_units
     ids_t, slots_t, combine_t = expert_ids.T, slots.T, combine.T
 
@@ -224,14 +226,14 @@
             pltpu.VMEM(slots_t.shape, jnp.int32),
             pltpu.VMEM((block, 2 * PACK * width + LANES), BF16),
             pltpu.SemaphoreType.DMA((5,)),
-            pltpu.SemaphoreType.DMA((2,)),
+            pltpu.SemaphoreType.DMA((2 * PACK,)),
         ],
         limit=60,
         ins="hhhhh",
         outs="h",
     )
     got = lax.all_to_all(sent, "expert", split_axis=0, concat_axis=0, tiled=True)
-    piece = shape(z_chips, chunk, cols)
+    piece = shape(high, chunk, cols)
     back, own, *pieces = call(
         expert_kernel,
         [shape(block, PACK * width + LANES)] + [piece] * len(FIRST),
@@ -241,18 +243,26 @@
             pltpu.VMEM((rows, width), BF16),
             pltpu.VMEM((rows, width), BF16),
             pltpu.VMEM((rows, cols), BF16),
-            pltpu.VMEM((width // chunk, chunk, cols), BF16),
+            pltpu.VMEM((high, len(FIRST), chunk, cols), BF16),
+            pltpu.VMEM((block, PACK * width + LANES), BF16),
+            pltpu.SemaphoreType.DMA,
         ],
-    )
+        outs="h",
+    )
+
+    def shift(values, dx, dz):
+        pairs = [
+            (z * X_CHIPS + x, (z + dz) % LOW * X_CHIPS + (x + dx) % X_CHIPS)
+            for z in range(LOW)
+            for x in range(X_CHIPS)
+        ]
+        return lax.ppermute(values, ("zl", "x"), pairs)
 
     returned = lax.all_to_all(back, "expert", split_axis=0, concat_axis=0, tiled=True)
-    arrived = [
-        lax.ppermute(values, "x", [(i, (i + dx) % X_CHIPS) for i in range(X_CHIPS)])
-        for values, dx in zip(pieces, FIRST[1:], strict=True)
-    ]
+    arrived = [shift(values, dx, dz) for values, (dx, dz) in zip(pieces, FIRST[1:], strict=True)]
     (summed,) = call(partial_kernel, [piece], (own, *arrived), limit=16)
     summed, returned = lax.optimization_barrier((summed, returned))
-    parts = lax.all_to_all(summed, "z", split_axis=0, concat_axis=0, tiled=True)
+    parts = lax.all_to_all(summed, "zh", split_axis=0, concat_axis=0, tiled=True)
     grad_tokens, grad_combine = call(
         functools.partial(combine_kernel, experts, per),
         [shape(tok_rows, width), shape(*ids_t.shape)],
@@ -265,8 +275,10 @@
 
 def solution(mesh):
     groups, experts = mesh.devices.shape
-    split = Mesh(mesh.devices.reshape(groups // X_CHIPS, X_CHIPS, experts), ("z", "x", "expert"))
-    dp = ("z", "x")
+    split = Mesh(
+        mesh.devices.reshape(groups // X_CHIPS // LOW, LOW, X_CHIPS, experts), ("zh", "zl", "x", "expert")
+    )
+    dp = ("zh", "zl", "x")
     rows = P((*dp, "expert"), None)
     weight = P("expert", None, None)
     return jax.shard_map(

time: 137 us -> 129 us (0.942)
  the two profiles are of different devices: /device:TPU:1 before, /device:TPU:8 now
where the time goes in v3:
time: 129 us
  blocking collectives  60.7 us (47%)
  starting transfers between devices  40.2 us (31%)
  waiting for transfers between devices  15.9 us (12%)
  Pallas kernels  11.4 us (9%)
    all_to_all x1, blocking collectives, shards(): lax.all_to_all(sent, 'expert', split_axis=0, concat_axis=0, tiled=True)  60.7 us
    ppermute x7, starting transfers between devices, shift(): return lax.ppermute(values, ('zl', 'x'), pairs)  25.7 us
    pallas_call x5, Pallas kernels, call(): pl.pallas_call(kernel, out_shape=out_shape, in_specs=specs(ins, len(args)...  11.4 us
    all_to_all x1, starting transfers between devices, shards(): lax.all_to_all(summed, 'zh', split_axis=0, concat_axis=0, tiled=True)  9.66 us
    all_to_all x1, waiting for transfers between devices, shards(): lax.all_to_all(summed, 'zh', split_axis=0, concat_axis=0, tiled=True)  8.43 us
    ppermute x7, waiting for transfers between devices, shift(): return lax.ppermute(values, ('zl', 'x'), pairs)  7.42 us
    all_to_all x1, starting transfers between devices, shards(): lax.all_to_all(back, 'expert', split_axis=0, concat_axis=0, tiled=True)  4.82 us
  transfers between devices with their start and end apart: 9, of which 3 were waited for; matrix products, arithmetic and copies ran while one was open for 0% of the time, Pallas kernels for 2%

profile of v3, /device:TPU:8, one launch (start us, length us, event | category | flops | bytes accessed | tf_op | source)
XLA Modules:
  0.0 128.9 jit_solution(9828460950241405176)
XLA Ops:
  0.6 3.1 %shard_map.119 = bf16[128,8320]{1,0:T(8,128)(2,1)} custom-call(bf16[256,1024]{1,0:T(8,128)(2,1)} %x_hbm.1, bf16[256,1024]{1,0:T(8,128)(2,1)} %g_hbm.1, bf16[8,256]{1,0:T(8,128)(2,1)} %bitcast.26, s32[8,256]{1,0:T(8,128)} %bitcast.18, s32[8,256]{1,0:T(8,128)} %bitcast.20), custom_call_target="tpu_custom_call" | custom-call | flops 536870912 | bytes 3198976 | tf_op jit(solution)/shard_map/pallas_call | solution.py:189
  3.8 0.0 copy-start.2
  3.8 0.0 copy-start.3
  3.8 0.0 copy-start.4
  3.8 60.7 %all_to_all.28 = bf16[16,8,8320]{2,1,0:T(8,128)(2,1)S(1)} all-to-all(bf16[16,8,8320]{2,1,0:T(8,128)(2,1)} %bitcast.25), channel_id=1, replica_groups=mesh['zh'=4,'zl'=2,'x'=4,'expert'=16] {'expert'}, dimensions={0} | all-to-all | bytes 4259840 | tf_op jit(solution)/shard_map/all_to_all | solution.py:235
  64.5 0.0 copy-done.2
  64.5 0.0 copy-done.3
  64.5 0.0 copy-done.4
  64.5 4.6 %shard_map.120 = (bf16[128,4224]{1,0:T(8,128)(2,1)}, bf16[4,32,1152]{2,1,0:T(8,128)(2,1)S(1)}, bf16[4,32,1152]{2,1,0:T(8,128)(2,1)S(1)}, bf16[4,32,1152]{2,1,0:T...) custom-call(bf16[128,8320]{1,0:T(8,128)(2,1)S(1)} %bitcast.17, ...), custom_call_target="tpu_custom_call" | custom-call | flops 3221225472 | bytes 7929856 | tf_op jit(solution)/shard_map/pallas_call | solution.py:189
  69.1 4.8 %all-to-all-start.1 = ((bf16[16,8,4224]{2,1,0:T(8,128)(2,1)}), bf16[16,8,4224]{2,1,0:T(8,128)(2,1)S(1)}, u32[]{:S(2)}, u32[]{:S(2)}) async-start(bf16[16,8,4224]{2,1,0:T(8,128)(2,1)} %bitcast.8), calls=%async_computation.1 | async-start | bytes 2162688 | tf_op jit(solution)/shard_map/all_to_all | solution.py:261
  73.9 0.0 copy-start
  73.9 0.0 copy-start.1
  73.9 4.9 %collective-permute-start = (bf16[4,32,1152]{2,1,0:T(8,128)(2,1)S(1)}, bf16[4,32,1152]{2,1,0:T(8,128)(2,1)S(1)}, u32[]{:S(2)}, u32[]{:S(2)}) collective-permute-start(bf16[4,32,1152]{2,1,0:T(8,128)(2,1)S(1)} %get-tuple-element.22), channel_id=1, source_target_pairs={{0,96},{16,112},{32,64},{48,80},{64,32},{80,48},{96,0},{112,16},{1... | collective-permute-start | bytes 884744 | tf_op jit(solution)/shard_map/ppermute | solution.py:259
  78.9 2.4 %collective-permute-start.1 = (bf16[4,32,1152]{2,1,0:T(8,128)(2,1)S(1)}, bf16[4,32,1152]{2,1,0:T(8,128)(2,1)S(1)}, u32[]{:S(2)}, u32[]{:S(2)}) collective-permute-start(bf16[4,32,1152]{2,1,0:T(8,128)(2,1)S(1)} %get-tuple-element.23), channel_id=1, source_target_pairs={{0,32},{16,48},{32,0},{48,16},{64,96},{80,112},{96,64},{112,80},{1... | collective-permute-start | bytes 884744 | tf_op jit(solution)/shard_map/ppermute | solution.py:259
  81.3 3.4 %collective-permute-start.2 = (bf16[4,32,1152]{2,1,0:T(8,128)(2,1)S(1)}, bf16[4,32,1152]{2,1,0:T(8,128)(2,1)S(1)}, u32[]{:S(2)}, u32[]{:S(2)}) collective-permute-start(bf16[4,32,1152]{2,1,0:T(8,128)(2,1)S(1)} %get-tuple-element.24), channel_id=1, source_target_pairs={{0,64},{16,80},{32,96},{48,112},{64,0},{80,16},{96,32},{112,48},{1... | collective-permute-start | bytes 884744 | tf_op jit(solution)/shard_map/ppermute | solution.py:259
  84.7 1.9 %collective-permute-start.3 = (bf16[4,32,1152]{2,1,0:T(8,128)(2,1)S(1)}, bf16[4,32,1152]{2,1,0:T(8,128)(2,1)S(1)}, u32[]{:S(2)}, u32[]{:S(2)}) collective-permute-start(bf16[4,32,1152]{2,1,0:T(8,128)(2,1)S(1)} %get-tuple-element.25), channel_id=1, source_target_pairs={{0,16},{16,32},{32,48},{48,0},{64,80},{80,96},{96,112},{112,64},{1... | collective-permute-start | bytes 884744 | tf_op jit(solution)/shard_map/ppermute | solution.py:259
  86.6 5.1 %collective-permute-start.4 = (bf16[4,32,1152]{2,1,0:T(8,128)(2,1)S(1)}, bf16[4,32,1152]{2,1,0:T(8,128)(2,1)S(1)}, u32[]{:S(2)}, u32[]{:S(2)}) collective-permute-start(bf16[4,32,1152]{2,1,0:T(8,128)(2,1)S(1)} %get-tuple-element.26), channel_id=1, source_target_pairs={{0,48},{16,0},{32,16},{48,32},{64,112},{80,64},{96,80},{112,96},{1... | collective-permute-start | bytes 884744 | tf_op jit(solution)/shard_map/ppermute | solution.py:259
  91.7 0.0 collective-permute-done.refs_1_
  91.7 2.2 %collective-permute-start.5 = (bf16[4,32,1152]{2,1,0:T(8,128)(2,1)S(1)}, bf16[4,32,1152]{2,1,0:T(8,128)(2,1)S(1)}, u32[]{:S(2)}, u32[]{:S(2)}) collective-permute-start(bf16[4,32,1152]{2,1,0:T(8,128)(2,1)S(1)} %get-tuple-element.27), channel_id=1, source_target_pairs={{0,80},{16,96},{32,112},{48,64},{64,16},{80,32},{96,48},{112,0},{1... | collective-permute-start | bytes 884744 | tf_op jit(solution)/shard_map/ppermute | solution.py:259
  93.9 0.0 collective-permute-done.1.refs_2_
  93.9 5.8 %collective-permute-start.6 = (bf16[4,32,1152]{2,1,0:T(8,128)(2,1)S(1)}, bf16[4,32,1152]{2,1,0:T(8,128)(2,1)S(1)}, u32[]{:S(2)}, u32[]{:S(2)}) collective-permute-start(bf16[4,32,1152]{2,1,0:T(8,128)(2,1)S(1)} %get-tuple-element.28), channel_id=1, source_target_pairs={{0,112},{16,64},{32,80},{48,96},{64,48},{80,0},{96,16},{112,32},{1... | collective-permute-start | bytes 884744 | tf_op jit(solution)/shard_map/ppermute | solution.py:259
  99.7 0.0 collective-permute-done.2.refs_3_
  99.7 6.5 %collective-permute-done.3.refs_4_ = bf16[4,32,1152]{2,1,0:T(8,128)(2,1)S(1)} collective-permute-done((bf16[4,32,1152]{2,1,0:T(8,128)(2,1)S(1)}, bf16[4,32,1152]{2,1,0:T(8,128)(2,1)S(1)}, u32[]{:S(2)}, u32[]{:S(2)}) %collective-permute-start.3) | collective-permute-done | bytes 294944 | tf_op jit(solution)/shard_map/ppermute | solution.py:259
  106.2 0.0 collective-permute-done.4.refs_5_
  106.2 0.0 collective-permute-done.5.refs_6_
  106.2 0.9 collective-permute-done.6.refs_7_
  107.1 1.0 shard_map.121
  108.2 0.0 all-to-all-done.1
  108.2 9.7 %all-to-all-start.2 = ((bf16[4,32,1152]{2,1,0:T(8,128)(2,1)}), bf16[4,32,1152]{2,1,0:T(8,128)(2,1)S(1)}, u32[]{:S(2)}, u32[]{:S(2)}) async-start(bf16[4,32,1152]{2,1,0:T(8,128)(2,1)} %shard_map.121), calls=%async_computation.2 | async-start | bytes 589824 | tf_op jit(solution)/shard_map/all_to_all | solution.py:265
  117.8 0.0 copy-done
  117.8 0.0 copy-done.1
  117.8 2.0 %shard_map.122 = (bf16[256,1024]{1,0:T(8,128)(2,1)}, bf16[8,256]{1,0:T(8,128)(2,1)}) custom-call(bf16[128,4224]{1,0:T(8,128)(2,1)S(1)} %bitcast.16, s32[8,256]{1,0:T(8,128)S(1)} %bitcast.19, s32[8,256]{1,0:T(8,128)S(1)} %bitcast.21), custom_call_target="tpu_custom_call" | custom-call | flops 268435456 | bytes 1626112 | tf_op jit(solution)/shard_map/pallas_call | solution.py:189
  119.8 8.4 %all-to-all-done.2.parts_ref = bf16[4,32,1152]{2,1,0:T(8,128)(2,1)S(1)} async-done(((bf16[4,32,1152]{2,1,0:T(8,128)(2,1)}), bf16[4,32,1152]{2,1,0:T(8,128)(2,1)S(1)}, u32[]{:S(2)}, u32[]{:S(2)}) %all-to-all-start.2) | async-done | bytes 294944 | tf_op jit(solution)/shard_map/all_to_all | solution.py:265
  128.3 0.7 shard_map.123
Async XLA Ops:
  3.8 60.7 %copy-start.2 = (bf16[1,1024,384]{2,1,0:T(8,128)(2,1)S(1)}, bf16[1,1024,384]{2,1,0:T(8,128)(2,1)}, u32[]{:S(2)}) copy-start(bf16[1,1024,384]{2,1,0:T(8,128)(2,1)} %param.13) | copy-start | bytes 2359300
  3.8 60.7 %copy-start.3 = (bf16[1,1024,384]{2,1,0:T(8,128)(2,1)S(1)}, bf16[1,1024,384]{2,1,0:T(8,128)(2,1)}, u32[]{:S(2)}) copy-start(bf16[1,1024,384]{2,1,0:T(8,128)(2,1)} %param.14) | copy-start | bytes 2359300
  3.8 60.7 %copy-start.4 = (bf16[1,384,1024]{2,1,0:T(8,128)(2,1)S(1)}, bf16[1,384,1024]{2,1,0:T(8,128)(2,1)}, u32[]{:S(2)}) copy-start(bf16[1,384,1024]{2,1,0:T(8,128)(2,1)} %param.15) | copy-start | bytes 2359300
  69.1 39.1 %all-to-all-start.1 = ((bf16[16,8,4224]{2,1,0:T(8,128)(2,1)}), bf16[16,8,4224]{2,1,0:T(8,128)(2,1)S(1)}, u32[]{:S(2)}, u32[]{:S(2)}) async-start(bf16[16,8,4224]{2,1,0:T(8,128)(2,1)} %bitcast.8), calls=%async_computation.1 | async-start | bytes 2162688 | tf_op jit(solution)/shard_map/all_to_all | solution.py:261
  73.9 43.9 %copy-start = (s32[256,8]{0,1:T(8,128)S(1)}, s32[256,8]{0,1:T(8,128)}, u32[]{:S(2)}) copy-start(s32[256,8]{0,1:T(8,128)} %param.11) | copy-start | bytes 24580
  73.9 43.9 %copy-start.1 = (s32[256,8]{0,1:T(8,128)S(1)}, s32[256,8]{0,1:T(8,128)}, u32[]{:S(2)}) copy-start(s32[256,8]{0,1:T(8,128)} %param.12) | copy-start | bytes 24580
  73.9 17.8 %collective-permute-start = (bf16[4,32,1152]{2,1,0:T(8,128)(2,1)S(1)}, bf16[4,32,1152]{2,1,0:T(8,128)(2,1)S(1)}, u32[]{:S(2)}, u32[]{:S(2)}) collective-permute-start(bf16[4,32,1152]{2,1,0:T(8,128)(2,1)S(1)} %get-tuple-element.22), channel_id=1, source_target_pairs={{0,96},{16,112},{32,64},{48,80},{64,32},{80,48},{96,0},{112,16},{1... | collective-permute-start | bytes 884744 | tf_op jit(solution)/shard_map/ppermute | solution.py:259
  78.9 15.1 %collective-permute-start.1 = (bf16[4,32,1152]{2,1,0:T(8,128)(2,1)S(1)}, bf16[4,32,1152]{2,1,0:T(8,128)(2,1)S(1)}, u32[]{:S(2)}, u32[]{:S(2)}) collective-permute-start(bf16[4,32,1152]{2,1,0:T(8,128)(2,1)S(1)} %get-tuple-element.23), channel_id=1, source_target_pairs={{0,32},{16,48},{32,0},{48,16},{64,96},{80,112},{96,64},{112,80},{1... | collective-permute-start | bytes 884744 | tf_op jit(solution)/shard_map/ppermute | solution.py:259
  81.3 18.4 %collective-permute-start.2 = (bf16[4,32,1152]{2,1,0:T(8,128)(2,1)S(1)}, bf16[4,32,1152]{2,1,0:T(8,128)(2,1)S(1)}, u32[]{:S(2)}, u32[]{:S(2)}) collective-permute-start(bf16[4,32,1152]{2,1,0:T(8,128)(2,1)S(1)} %get-tuple-element.24), channel_id=1, source_target_pairs={{0,64},{16,80},{32,96},{48,112},{64,0},{80,16},{96,32},{112,48},{1... | collective-permute-start | bytes 884744 | tf_op jit(solution)/shard_map/ppermute | solution.py:259
  84.7 21.6 %collective-permute-start.3 = (bf16[4,32,1152]{2,1,0:T(8,128)(2,1)S(1)}, bf16[4,32,1152]{2,1,0:T(8,128)(2,1)S(1)}, u32[]{:S(2)}, u32[]{:S(2)}) collective-permute-start(bf16[4,32,1152]{2,1,0:T(8,128)(2,1)S(1)} %get-tuple-element.25), channel_id=1, source_target_pairs={{0,16},{16,32},{32,48},{48,0},{64,80},{80,96},{96,112},{112,64},{1... | collective-permute-start | bytes 884744 | tf_op jit(solution)/shard_map/ppermute | solution.py:259
  86.6 19.6 %collective-permute-start.4 = (bf16[4,32,1152]{2,1,0:T(8,128)(2,1)S(1)}, bf16[4,32,1152]{2,1,0:T(8,128)(2,1)S(1)}, u32[]{:S(2)}, u32[]{:S(2)}) collective-permute-start(bf16[4,32,1152]{2,1,0:T(8,128)(2,1)S(1)} %get-tuple-element.26), channel_id=1, source_target_pairs={{0,48},{16,0},{32,16},{48,32},{64,112},{80,64},{96,80},{112,96},{1... | collective-permute-start | bytes 884744 | tf_op jit(solution)/shard_map/ppermute | solution.py:259
  91.7 14.5 %collective-permute-start.5 = (bf16[4,32,1152]{2,1,0:T(8,128)(2,1)S(1)}, bf16[4,32,1152]{2,1,0:T(8,128)(2,1)S(1)}, u32[]{:S(2)}, u32[]{:S(2)}) collective-permute-start(bf16[4,32,1152]{2,1,0:T(8,128)(2,1)S(1)} %get-tuple-element.27), channel_id=1, source_target_pairs={{0,80},{16,96},{32,112},{48,64},{64,16},{80,32},{96,48},{112,0},{1... | collective-permute-start | bytes 884744 | tf_op jit(solution)/shard_map/ppermute | solution.py:259
  93.9 13.2 %collective-permute-start.6 = (bf16[4,32,1152]{2,1,0:T(8,128)(2,1)S(1)}, bf16[4,32,1152]{2,1,0:T(8,128)(2,1)S(1)}, u32[]{:S(2)}, u32[]{:S(2)}) collective-permute-start(bf16[4,32,1152]{2,1,0:T(8,128)(2,1)S(1)} %get-tuple-element.28), channel_id=1, source_target_pairs={{0,112},{16,64},{32,80},{48,96},{64,48},{80,0},{96,16},{112,32},{1... | collective-permute-start | bytes 884744 | tf_op jit(solution)/shard_map/ppermute | solution.py:259
  108.2 20.1 %all-to-all-start.2 = ((bf16[4,32,1152]{2,1,0:T(8,128)(2,1)}), bf16[4,32,1152]{2,1,0:T(8,128)(2,1)S(1)}, u32[]{:S(2)}, u32[]{:S(2)}) async-start(bf16[4,32,1152]{2,1,0:T(8,128)(2,1)} %shard_map.121), calls=%async_computation.2 | async-start | bytes 589824 | tf_op jit(solution)/shard_map/all_to_all | solution.py:265

commit v4 on v3

--- a/solution.py
+++ b/solution.py
@@ -48,40 +48,46 @@
         fetch.wait()
     pos = positions(id_ref[...], slot_ref[...], experts, per)
     weights = c_ref[...].astype(F32)
-    index = lax.broadcasted_iota(jnp.int32, (rows, tokens), 0)
-    routed = jnp.zeros((rows, tokens), F32)
-    scaled = jnp.zeros((rows, tokens), F32)
-    for k in range(pos.shape[0]):
-        match = index == pos[k : k + 1, :]
-        routed = jnp.where(match, 1.0, routed)
-        scaled = jnp.where(match, weights[k : k + 1, :], scaled)
-    routed = routed.astype(BF16)
-    code = jnp.sum(scaled, axis=1, keepdims=True)
+    index = lax.broadcasted_iota(jnp.int32, (block, tokens), 0)
     lane = lax.broadcasted_iota(jnp.int32, (block, LANES), 1)
     coded = jnp.zeros((block, LANES), F32)
-    for q in range(PACK):
-        coded = jnp.where(lane // CODE == q, code[q * block : (q + 1) * block], coded)
+    picks, sends = [], []
+
+    def send(lo, hi):
+        copy = pltpu.make_async_copy(out_ref.at[:, lo:hi], out_hbm.at[:, lo:hi], out_sems.at[len(sends)])
+        copy.start()
+        sends.append(copy)
+
+    for q in range(PACK):
+        routed = jnp.zeros((block, tokens), F32)
+        scaled = jnp.zeros((block, tokens), F32)
+        for k in range(pos.shape[0]):
+            match = index + q * block == pos[k : k + 1, :]
+            routed = jnp.where(match, 1.0, routed)
+            scaled = jnp.where(match, weights[k : k + 1, :], scaled)
+        picks.append(routed.astype(BF16))
+        coded = jnp.where(lane // CODE == q, jnp.sum(scaled, axis=1, keepdims=True), coded)
+        if q == 0:
+            fetch_x.wait()
+        out_ref[:, q * width : (q + 1) * width] = dot(picks[q], x_ref[...]).astype(BF16)
+        send(q * width, (q + 1) * width)
     out_ref[:, 2 * PACK * width :] = coded.astype(BF16)
-    fetch_x.wait()
-    sends = []
-    for i, (fetch, ref) in enumerate(((None, x_ref), (fetch_g, g_ref))):
-        if fetch is not None:
-            fetch.wait()
-        for q in range(PACK):
-            lo = (i * PACK + q) * width
-            hi = lo + width if (i, q) != (1, PACK - 1) else out_ref.shape[1]
-            out_ref[:, lo : lo + width] = dot(routed[q * block : (q + 1) * block], ref[...]).astype(BF16)
-            sends.append(pltpu.make_async_copy(out_ref.at[:, lo:hi], out_hbm.at[:, lo:hi], out_sems.at[len(sends)]))
-            sends[-1].start()
-    for send in sends:
-        send.wait()
+    fetch_g.wait()
+    for q in range(PACK):
+        lo = (PACK + q) * width
+        out_ref[:, lo : lo + width] = dot(picks[q], g_ref[...]).astype(BF16)
+        send(lo, lo + width if q < PACK - 1 else out_ref.shape[1])
+    for copy in sends:
+        copy.wait()
 
 
 def expert_kernel(rows_ref, wg_ref, wu_ref, wd_ref, back_hbm, *rest):
-    pieces, (x_all, g_all, act_all, part, back_ref, sem) = rest[:-6], rest[-6:]
+    pieces, (wgu_ref, x_all, g_all, act_all, part, back_ref, sem) = rest[:-7], rest[-7:]
     block = back_ref.shape[0]
     hidden_units, width = wd_ref.shape
     rows = PACK * block
+    wgu_ref[:, :hidden_units] = wg_ref[...]
+    wgu_ref[:, hidden_units:] = wu_ref[...]
     for q in range(PACK):
         x_all[q * block : (q + 1) * block, :] = rows_ref[:, q * width : (q + 1) * width]
         g_all[q * block : (q + 1) * block, :] = rows_ref[:, (PACK + q) * width : (PACK + q + 1) * width]
@@ -98,8 +104,8 @@
             ],
             axis=0,
         )
-        gate = dot(x_all[lo:hi, :], wg_ref[...])
-        up = dot(x_all[lo:hi, :], wu_ref[...])
+        pre = dot(x_all[lo:hi, :], wgu_ref[...])
+        gate, up = pre[:, :hidden_units], pre[:, hidden_units:]
         sig = 1.0 / (1.0 + jnp.exp(-gate))
         act = gate * sig
         hidden = (act * up).astype(BF16)
@@ -113,14 +119,14 @@
         act_all[lo:hi, hidden_units : 2 * hidden_units] = (grad_hidden * act).astype(BF16)
         act_all[lo:hi, 2 * hidden_units :] = hidden
     back_ref[:, PACK * width :] = sums.astype(BF16)
-    grad = dot(act_all[:, :hidden_units], wg_ref[...], NT)
-    grad = (grad + dot(act_all[:, hidden_units : 2 * hidden_units], wu_ref[...], NT)).astype(BF16)
+    grad = dot(act_all[:, : 2 * hidden_units], wgu_ref[...], NT).astype(BF16)
     for q in range(PACK):
         back_ref[:, q * width : (q + 1) * width] = grad[q * block : (q + 1) * block]
     store = pltpu.make_async_copy(back_ref, back_hbm, sem)
     store.start()
     x_here, low_here = lax.axis_index("x"), lax.axis_index("zl")
-    places = [lax.rem(low_here + dz, LOW) * X_CHIPS + lax.rem(x_here + dx, X_CHIPS) for dx, dz in FIRST]
+    flips = (x_here, x_here + 1 - 2 * lax.rem(x_here, 2), lax.rem(x_here + 2, X_CHIPS), X_CHIPS - 1 - x_here)
+    places = [lax.rem(low_here + dz, LOW) * X_CHIPS + flips[dx] for dx, dz in FIRST]
     chunk = part.shape[2]
     step = chunk * len(FIRST)
     for z in range(width // step):
@@ -136,10 +142,17 @@
 
 
 def partial_kernel(*refs):
-    total = refs[0][...].astype(F32)
-    for ref in refs[1:-1]:
-        total = total + ref[...].astype(F32)
-    refs[-1][...] = total.astype(BF16)
+    parts, (out_hbm, out_ref, sems) = refs[:-3], refs[-3:]
+    stores = []
+    for z in range(out_ref.shape[0]):
+        total = parts[0][z].astype(F32)
+        for ref in parts[1:]:
+            total = total + ref[z].astype(F32)
+        out_ref[z] = total.astype(BF16)
+        stores.append(pltpu.make_async_copy(out_ref.at[z], out_hbm.at[z], sems.at[z]))
+        stores[-1].start()
+    for store in stores:
+        store.wait()
 
 
 def combine_kernel(experts, per, back_ref, id_ref, slot_ref, grad_ref, comb_ref):
@@ -240,6 +253,7 @@
         (got, w_gate[0], w_up[0], w_down[0]),
         flops=16 * rows * width * hidden_units,
         scratch=[
+            pltpu.VMEM((width, 2 * hidden_units), BF16),
             pltpu.VMEM((rows, width), BF16),
             pltpu.VMEM((rows, width), BF16),
             pltpu.VMEM((rows, cols), BF16),
@@ -252,7 +266,7 @@
 
     def shift(values, dx, dz):
         pairs = [
-            (z * X_CHIPS + x, (z + dz) % LOW * X_CHIPS + (x + dx) % X_CHIPS)
+            (z * X_CHIPS + x, (z ^ dz) * X_CHIPS + (x ^ dx))
             for z in range(LOW)
             for x in range(X_CHIPS)
         ]
@@ -260,7 +274,14 @@
 
     returned = lax.all_to_all(back, "expert", split_axis=0, concat_axis=0, tiled=True)
     arrived = [shift(values, dx, dz) for values, (dx, dz) in zip(pieces, FIRST[1:], strict=True)]
-    (summed,) = call(partial_kernel, [piece], (own, *arrived), limit=16)
+    (summed,) = call(
+        partial_kernel,
+        [piece],
+        (own, *arrived),
+        scratch=[pltpu.VMEM(piece.shape, BF16), pltpu.SemaphoreType.DMA((high,))],
+        limit=16,
+        outs="h",
+    )
     summed, returned = lax.optimization_barrier((summed, returned))
     parts = lax.all_to_all(summed, "zh", split_axis=0, concat_axis=0, tiled=True)
     grad_tokens, grad_combine = call(

time: 129 us -> 129 us (level)
  the two profiles are of different devices: /device:TPU:8 before, /device:TPU:14 now
where the time goes in v4:
time: 129 us; the launch traced here: 128 us
  blocking collectives  58.9 us (46%)
  starting transfers between devices  38.8 us (30%)
  waiting for transfers between devices  19.1 us (15%)
  Pallas kernels  10.8 us (8%)
    all_to_all x1, blocking collectives, shards(): lax.all_to_all(sent, 'expert', split_axis=0, concat_axis=0, tiled=True)  58.9 us
    ppermute x7, starting transfers between devices, shift(): return lax.ppermute(values, ('zl', 'x'), pairs)  24.3 us
    pallas_call x5, Pallas kernels, call(): pl.pallas_call(kernel, out_shape=out_shape, in_specs=specs(ins, len(args)...  10.8 us
    ppermute x7, waiting for transfers between devices, shift(): return lax.ppermute(values, ('zl', 'x'), pairs)  10.3 us
    all_to_all x1, starting transfers between devices, shards(): lax.all_to_all(summed, 'zh', split_axis=0, concat_axis=0, tiled=True)  9.67 us
    all_to_all x1, waiting for transfers between devices, shards(): lax.all_to_all(summed, 'zh', split_axis=0, concat_axis=0, tiled=True)  8.76 us
    all_to_all x1, starting transfers between devices, shards(): lax.all_to_all(back, 'expert', split_axis=0, concat_axis=0, tiled=True)  4.83 us
  transfers between devices with their start and end apart: 9, of which 3 were waited for; matrix products, arithmetic and copies ran while one was open for 0% of the time, Pallas kernels for 2%

profile of v4, /device:TPU:14, one launch (start us, length us, event | category | flops | bytes accessed | tf_op | source)
XLA Modules:
  0.0 128.4 jit_solution(10672268202333315656)
XLA Ops:
  0.6 3.1 %shard_map.119 = bf16[128,8320]{1,0:T(8,128)(2,1)} custom-call(bf16[256,1024]{1,0:T(8,128)(2,1)} %x_hbm.1, bf16[256,1024]{1,0:T(8,128)(2,1)} %g_hbm.1, bf16[8,256]{1,0:T(8,128)(2,1)} %bitcast.26, s32[8,256]{1,0:T(8,128)} %bitcast.18, s32[8,256]{1,0:T(8,128)} %bitcast.20), custom_call_target="tpu_custom_call" | custom-call | flops 536870912 | bytes 3198976 | tf_op jit(solution)/shard_map/pallas_call | solution.py:202
  3.7 0.0 copy-start.2
  3.8 0.0 copy-start.3
  3.8 0.0 copy-start.4
  3.8 58.9 %all_to_all.28 = bf16[16,8,8320]{2,1,0:T(8,128)(2,1)S(1)} all-to-all(bf16[16,8,8320]{2,1,0:T(8,128)(2,1)} %bitcast.25), channel_id=1, replica_groups=mesh['zh'=4,'zl'=2,'x'=4,'expert'=16] {'expert'}, dimensions={0} | all-to-all | bytes 4259840 | tf_op jit(solution)/shard_map/all_to_all | solution.py:248
  62.7 0.0 copy-done.2
  62.7 0.0 copy-done.3
  62.7 0.0 copy-done.4
  62.7 4.1 %shard_map.120 = (bf16[128,4224]{1,0:T(8,128)(2,1)}, bf16[4,32,1152]{2,1,0:T(8,128)(2,1)S(1)}, bf16[4,32,1152]{2,1,0:T(8,128)(2,1)S(1)}, bf16[4,32,1152]{2,1,0:T...) custom-call(bf16[128,8320]{1,0:T(8,128)(2,1)S(1)} %bitcast.17, ...), custom_call_target="tpu_custom_call" | custom-call | flops 3221225472 | bytes 7929856 | tf_op jit(solution)/shard_map/pallas_call | solution.py:202
  66.8 4.8 %all-to-all-start.1 = ((bf16[16,8,4224]{2,1,0:T(8,128)(2,1)}), bf16[16,8,4224]{2,1,0:T(8,128)(2,1)S(1)}, u32[]{:S(2)}, u32[]{:S(2)}) async-start(bf16[16,8,4224]{2,1,0:T(8,128)(2,1)} %bitcast.8), calls=%async_computation.1 | async-start | bytes 2162688 | tf_op jit(solution)/shard_map/all_to_all | solution.py:275
  71.6 0.0 copy-start
  71.6 0.0 copy-start.1
  71.6 5.1 %collective-permute-start = (bf16[4,32,1152]{2,1,0:T(8,128)(2,1)S(1)}, bf16[4,32,1152]{2,1,0:T(8,128)(2,1)S(1)}, u32[]{:S(2)}, u32[]{:S(2)}) collective-permute-start(bf16[4,32,1152]{2,1,0:T(8,128)(2,1)S(1)} %get-tuple-element.22), channel_id=1, source_target_pairs={{0,96},{16,112},{32,64},{48,80},{64,32},{80,48},{96,0},{112,16},{1... | collective-permute-start | bytes 884744 | tf_op jit(solution)/shard_map/ppermute | solution.py:273
  76.7 4.0 %collective-permute-start.1 = (bf16[4,32,1152]{2,1,0:T(8,128)(2,1)S(1)}, bf16[4,32,1152]{2,1,0:T(8,128)(2,1)S(1)}, u32[]{:S(2)}, u32[]{:S(2)}) collective-permute-start(bf16[4,32,1152]{2,1,0:T(8,128)(2,1)S(1)} %get-tuple-element.23), channel_id=1, source_target_pairs={{0,32},{16,48},{32,0},{48,16},{64,96},{80,112},{96,64},{112,80},{1... | collective-permute-start | bytes 884744 | tf_op jit(solution)/shard_map/ppermute | solution.py:273
  80.8 1.9 %collective-permute-start.2 = (bf16[4,32,1152]{2,1,0:T(8,128)(2,1)S(1)}, bf16[4,32,1152]{2,1,0:T(8,128)(2,1)S(1)}, u32[]{:S(2)}, u32[]{:S(2)}) collective-permute-start(bf16[4,32,1152]{2,1,0:T(8,128)(2,1)S(1)} %get-tuple-element.24), channel_id=1, source_target_pairs={{0,64},{16,80},{32,96},{48,112},{64,0},{80,16},{96,32},{112,48},{1... | collective-permute-start | bytes 884744 | tf_op jit(solution)/shard_map/ppermute | solution.py:273
  82.7 2.8 %collective-permute-start.3 = (bf16[4,32,1152]{2,1,0:T(8,128)(2,1)S(1)}, bf16[4,32,1152]{2,1,0:T(8,128)(2,1)S(1)}, u32[]{:S(2)}, u32[]{:S(2)}) collective-permute-start(bf16[4,32,1152]{2,1,0:T(8,128)(2,1)S(1)} %get-tuple-element.25), channel_id=1, source_target_pairs={{0,16},{16,0},{32,48},{48,32},{64,80},{80,64},{96,112},{112,96},{1... | collective-permute-start | bytes 884744 | tf_op jit(solution)/shard_map/ppermute | solution.py:273
  85.5 3.0 %collective-permute-start.4 = (bf16[4,32,1152]{2,1,0:T(8,128)(2,1)S(1)}, bf16[4,32,1152]{2,1,0:T(8,128)(2,1)S(1)}, u32[]{:S(2)}, u32[]{:S(2)}) collective-permute-start(bf16[4,32,1152]{2,1,0:T(8,128)(2,1)S(1)} %get-tuple-element.26), channel_id=1, source_target_pairs={{0,48},{16,32},{32,16},{48,0},{64,112},{80,96},{96,80},{112,64},{1... | collective-permute-start | bytes 884744 | tf_op jit(solution)/shard_map/ppermute | solution.py:273
  88.5 0.0 collective-permute-done.refs_1_
  88.5 3.4 %collective-permute-start.5 = (bf16[4,32,1152]{2,1,0:T(8,128)(2,1)S(1)}, bf16[4,32,1152]{2,1,0:T(8,128)(2,1)S(1)}, u32[]{:S(2)}, u32[]{:S(2)}) collective-permute-start(bf16[4,32,1152]{2,1,0:T(8,128)(2,1)S(1)} %get-tuple-element.27), channel_id=1, source_target_pairs={{0,80},{16,64},{32,112},{48,96},{64,16},{80,0},{96,48},{112,32},{1... | collective-permute-start | bytes 884744 | tf_op jit(solution)/shard_map/ppermute | solution.py:273
  92.0 0.0 collective-permute-done.1.refs_2_
  92.0 4.0 %collective-permute-start.6 = (bf16[4,32,1152]{2,1,0:T(8,128)(2,1)S(1)}, bf16[4,32,1152]{2,1,0:T(8,128)(2,1)S(1)}, u32[]{:S(2)}, u32[]{:S(2)}) collective-permute-start(bf16[4,32,1152]{2,1,0:T(8,128)(2,1)S(1)} %get-tuple-element.28), channel_id=1, source_target_pairs={{0,112},{16,96},{32,80},{48,64},{64,48},{80,32},{96,16},{112,0},{1... | collective-permute-start | bytes 884744 | tf_op jit(solution)/shard_map/ppermute | solution.py:273
  96.0 0.0 collective-permute-done.2.refs_3_
  96.0 7.6 %collective-permute-done.3.refs_4_ = bf16[4,32,1152]{2,1,0:T(8,128)(2,1)S(1)} collective-permute-done((bf16[4,32,1152]{2,1,0:T(8,128)(2,1)S(1)}, bf16[4,32,1152]{2,1,0:T(8,128)(2,1)S(1)}, u32[]{:S(2)}, u32[]{:S(2)}) %collective-permute-start.3) | collective-permute-done | bytes 294944 | tf_op jit(solution)/shard_map/ppermute | solution.py:273
  103.6 0.0 collective-permute-done.4.refs_5_
  103.6 0.0 collective-permute-done.5.refs_6_
  103.6 2.7 %collective-permute-done.6.refs_7_ = bf16[4,32,1152]{2,1,0:T(8,128)(2,1)S(1)} collective-permute-done((bf16[4,32,1152]{2,1,0:T(8,128)(2,1)S(1)}, bf16[4,32,1152]{2,1,0:T(8,128)(2,1)S(1)}, u32[]{:S(2)}, u32[]{:S(2)}) %collective-permute-start.6) | collective-permute-done | bytes 294944 | tf_op jit(solution)/shard_map/ppermute | solution.py:273
  106.3 1.0 shard_map.121
  107.3 0.0 all-to-all-done.1
  107.3 9.7 %all-to-all-start.2 = ((bf16[4,32,1152]{2,1,0:T(8,128)(2,1)}), bf16[4,32,1152]{2,1,0:T(8,128)(2,1)S(1)}, u32[]{:S(2)}, u32[]{:S(2)}) async-start(bf16[4,32,1152]{2,1,0:T(8,128)(2,1)} %shard_map.121), calls=%async_computation.2 | async-start | bytes 589824 | tf_op jit(solution)/shard_map/all_to_all | solution.py:286
  116.9 0.0 copy-done
  116.9 0.0 copy-done.1
  116.9 2.0 %shard_map.122 = (bf16[256,1024]{1,0:T(8,128)(2,1)}, bf16[8,256]{1,0:T(8,128)(2,1)}) custom-call(bf16[128,4224]{1,0:T(8,128)(2,1)S(1)} %bitcast.16, s32[8,256]{1,0:T(8,128)S(1)} %bitcast.19, s32[8,256]{1,0:T(8,128)S(1)} %bitcast.21), custom_call_target="tpu_custom_call" | custom-call | flops 268435456 | bytes 1626112 | tf_op jit(solution)/shard_map/pallas_call | solution.py:202
  118.9 8.8 %all-to-all-done.2.parts_ref = bf16[4,32,1152]{2,1,0:T(8,128)(2,1)S(1)} async-done(((bf16[4,32,1152]{2,1,0:T(8,128)(2,1)}), bf16[4,32,1152]{2,1,0:T(8,128)(2,1)S(1)}, u32[]{:S(2)}, u32[]{:S(2)}) %all-to-all-start.2) | async-done | bytes 294944 | tf_op jit(solution)/shard_map/all_to_all | solution.py:286
  127.7 0.7 shard_map.123
Async XLA Ops:
  3.7 58.9 %copy-start.2 = (bf16[1,1024,384]{2,1,0:T(8,128)(2,1)S(1)}, bf16[1,1024,384]{2,1,0:T(8,128)(2,1)}, u32[]{:S(2)}) copy-start(bf16[1,1024,384]{2,1,0:T(8,128)(2,1)} %param.13) | copy-start | bytes 2359300
  3.8 58.9 %copy-start.3 = (bf16[1,1024,384]{2,1,0:T(8,128)(2,1)S(1)}, bf16[1,1024,384]{2,1,0:T(8,128)(2,1)}, u32[]{:S(2)}) copy-start(bf16[1,1024,384]{2,1,0:T(8,128)(2,1)} %param.14) | copy-start | bytes 2359300
  3.8 58.9 %copy-start.4 = (bf16[1,384,1024]{2,1,0:T(8,128)(2,1)S(1)}, bf16[1,384,1024]{2,1,0:T(8,128)(2,1)}, u32[]{:S(2)}) copy-start(bf16[1,384,1024]{2,1,0:T(8,128)(2,1)} %param.15) | copy-start | bytes 2359300
  66.8 40.5 %all-to-all-start.1 = ((bf16[16,8,4224]{2,1,0:T(8,128)(2,1)}), bf16[16,8,4224]{2,1,0:T(8,128)(2,1)S(1)}, u32[]{:S(2)}, u32[]{:S(2)}) async-start(bf16[16,8,4224]{2,1,0:T(8,128)(2,1)} %bitcast.8), calls=%async_computation.1 | async-start | bytes 2162688 | tf_op jit(solution)/shard_map/all_to_all | solution.py:275
  71.6 45.4 %copy-start = (s32[256,8]{0,1:T(8,128)S(1)}, s32[256,8]{0,1:T(8,128)}, u32[]{:S(2)}) copy-start(s32[256,8]{0,1:T(8,128)} %param.11) | copy-start | bytes 24580
  71.6 45.3 %copy-start.1 = (s32[256,8]{0,1:T(8,128)S(1)}, s32[256,8]{0,1:T(8,128)}, u32[]{:S(2)}) copy-start(s32[256,8]{0,1:T(8,128)} %param.12) | copy-start | bytes 24580
  71.6 16.9 %collective-permute-start = (bf16[4,32,1152]{2,1,0:T(8,128)(2,1)S(1)}, bf16[4,32,1152]{2,1,0:T(8,128)(2,1)S(1)}, u32[]{:S(2)}, u32[]{:S(2)}) collective-permute-start(bf16[4,32,1152]{2,1,0:T(8,128)(2,1)S(1)} %get-tuple-element.22), channel_id=1, source_target_pairs={{0,96},{16,112},{32,64},{48,80},{64,32},{80,48},{96,0},{112,16},{1... | collective-permute-start | bytes 884744 | tf_op jit(solution)/shard_map/ppermute | solution.py:273
  76.7 15.2 %collective-permute-start.1 = (bf16[4,32,1152]{2,1,0:T(8,128)(2,1)S(1)}, bf16[4,32,1152]{2,1,0:T(8,128)(2,1)S(1)}, u32[]{:S(2)}, u32[]{:S(2)}) collective-permute-start(bf16[4,32,1152]{2,1,0:T(8,128)(2,1)S(1)} %get-tuple-element.23), channel_id=1, source_target_pairs={{0,32},{16,48},{32,0},{48,16},{64,96},{80,112},{96,64},{112,80},{1... | collective-permute-start | bytes 884744 | tf_op jit(solution)/shard_map/ppermute | solution.py:273
  80.8 15.2 %collective-permute-start.2 = (bf16[4,32,1152]{2,1,0:T(8,128)(2,1)S(1)}, bf16[4,32,1152]{2,1,0:T(8,128)(2,1)S(1)}, u32[]{:S(2)}, u32[]{:S(2)}) collective-permute-start(bf16[4,32,1152]{2,1,0:T(8,128)(2,1)S(1)} %get-tuple-element.24), channel_id=1, source_target_pairs={{0,64},{16,80},{32,96},{48,112},{64,0},{80,16},{96,32},{112,48},{1... | collective-permute-start | bytes 884744 | tf_op jit(solution)/shard_map/ppermute | solution.py:273
  82.7 20.9 %collective-permute-start.3 = (bf16[4,32,1152]{2,1,0:T(8,128)(2,1)S(1)}, bf16[4,32,1152]{2,1,0:T(8,128)(2,1)S(1)}, u32[]{:S(2)}, u32[]{:S(2)}) collective-permute-start(bf16[4,32,1152]{2,1,0:T(8,128)(2,1)S(1)} %get-tuple-element.25), channel_id=1, source_target_pairs={{0,16},{16,0},{32,48},{48,32},{64,80},{80,64},{96,112},{112,96},{1... | collective-permute-start | bytes 884744 | tf_op jit(solution)/shard_map/ppermute | solution.py:273
  85.5 18.1 %collective-permute-start.4 = (bf16[4,32,1152]{2,1,0:T(8,128)(2,1)S(1)}, bf16[4,32,1152]{2,1,0:T(8,128)(2,1)S(1)}, u32[]{:S(2)}, u32[]{:S(2)}) collective-permute-start(bf16[4,32,1152]{2,1,0:T(8,128)(2,1)S(1)} %get-tuple-element.26), channel_id=1, source_target_pairs={{0,48},{16,32},{32,16},{48,0},{64,112},{80,96},{96,80},{112,64},{1... | collective-permute-start | bytes 884744 | tf_op jit(solution)/shard_map/ppermute | solution.py:273
  88.5 15.1 %collective-permute-start.5 = (bf16[4,32,1152]{2,1,0:T(8,128)(2,1)S(1)}, bf16[4,32,1152]{2,1,0:T(8,128)(2,1)S(1)}, u32[]{:S(2)}, u32[]{:S(2)}) collective-permute-start(bf16[4,32,1152]{2,1,0:T(8,128)(2,1)S(1)} %get-tuple-element.27), channel_id=1, source_target_pairs={{0,80},{16,64},{32,112},{48,96},{64,16},{80,0},{96,48},{112,32},{1... | collective-permute-start | bytes 884744 | tf_op jit(solution)/shard_map/ppermute | solution.py:273
  92.0 14.3 %collective-permute-start.6 = (bf16[4,32,1152]{2,1,0:T(8,128)(2,1)S(1)}, bf16[4,32,1152]{2,1,0:T(8,128)(2,1)S(1)}, u32[]{:S(2)}, u32[]{:S(2)}) collective-permute-start(bf16[4,32,1152]{2,1,0:T(8,128)(2,1)S(1)} %get-tuple-element.28), channel_id=1, source_target_pairs={{0,112},{16,96},{32,80},{48,64},{64,48},{80,32},{96,16},{112,0},{1... | collective-permute-start | bytes 884744 | tf_op jit(solution)/shard_map/ppermute | solution.py:273
  107.3 20.4 %all-to-all-start.2 = ((bf16[4,32,1152]{2,1,0:T(8,128)(2,1)}), bf16[4,32,1152]{2,1,0:T(8,128)(2,1)S(1)}, u32[]{:S(2)}, u32[]{:S(2)}) async-start(bf16[4,32,1152]{2,1,0:T(8,128)(2,1)} %shard_map.121), calls=%async_computation.2 | async-start | bytes 589824 | tf_op jit(solution)/shard_map/all_to_all | solution.py:286

commit v5 on v4

--- a/solution.py
+++ b/solution.py
@@ -12,7 +12,7 @@
 PACK = 4
 CODE = LANES // PACK
 LOW = 2
-FIRST = ((0, 0), (2, 1), (2, 0), (0, 1), (1, 0), (3, 0), (1, 1), (3, 1))
+FIRST = ((0, 0), (2, 1), (2, 0), (0, 1), (3, 0), (1, 1), (1, 0), (3, 1))
 F32 = jnp.float32
 BF16 = jnp.bfloat16
 NN = (((1,), (0,)), ((), ()))

time: 129 us -> 129 us (level)
  the two profiles are of different devices: /device:TPU:14 before, /device:TPU:8 now
where the time goes in v5:
time: 129 us; the launch traced here: 128 us
  blocking collectives  60.7 us (47%)
  starting transfers between devices  38.7 us (30%)
  waiting for transfers between devices  17 us (13%)
  Pallas kernels  10.8 us (8%)
    all_to_all x1, blocking collectives, shards(): lax.all_to_all(sent, 'expert', split_axis=0, concat_axis=0, tiled=True)  60.7 us
    ppermute x7, starting transfers between devices, shift(): return lax.ppermute(values, ('zl', 'x'), pairs)  24.5 us
    pallas_call x5, Pallas kernels, call(): pl.pallas_call(kernel, out_shape=out_shape, in_specs=specs(ins, len(args)...  10.8 us
    all_to_all x1, starting transfers between devices, shards(): lax.all_to_all(summed, 'zh', split_axis=0, concat_axis=0, tiled=True)  9.41 us
    all_to_all x1, waiting for transfers between devices, shards(): lax.all_to_all(summed, 'zh', split_axis=0, concat_axis=0, tiled=True)  8.92 us
    ppermute x7, waiting for transfers between devices, shift(): return lax.ppermute(values, ('zl', 'x'), pairs)  8.07 us
    all_to_all x1, starting transfers between devices, shards(): lax.all_to_all(back, 'expert', split_axis=0, concat_axis=0, tiled=True)  4.81 us
  transfers between devices with their start and end apart: 9, of which 4 were waited for; matrix products, arithmetic and copies ran while one was open for 0% of the time, Pallas kernels for 2%

profile of v5, /device:TPU:8, one launch (start us, length us, event | category | flops | bytes accessed | tf_op | source)
XLA Modules:
  0.0 128.1 jit_solution(1468032011532238712)
XLA Ops:
  0.6 3.1 %shard_map.119 = bf16[128,8320]{1,0:T(8,128)(2,1)} custom-call(bf16[256,1024]{1,0:T(8,128)(2,1)} %x_hbm.1, bf16[256,1024]{1,0:T(8,128)(2,1)} %g_hbm.1, bf16[8,256]{1,0:T(8,128)(2,1)} %bitcast.26, s32[8,256]{1,0:T(8,128)} %bitcast.18, s32[8,256]{1,0:T(8,128)} %bitcast.20), custom_call_target="tpu_custom_call" | custom-call | flops 536870912 | bytes 3198976 | tf_op jit(solution)/shard_map/pallas_call | solution.py:202
  3.7 0.0 copy-start.2
  3.8 0.0 copy-start.3
  3.8 0.0 copy-start.4
  3.8 60.7 %all_to_all.28 = bf16[16,8,8320]{2,1,0:T(8,128)(2,1)S(1)} all-to-all(bf16[16,8,8320]{2,1,0:T(8,128)(2,1)} %bitcast.25), channel_id=1, replica_groups=mesh['zh'=4,'zl'=2,'x'=4,'expert'=16] {'expert'}, dimensions={0} | all-to-all | bytes 4259840 | tf_op jit(solution)/shard_map/all_to_all | solution.py:248
  64.5 0.0 copy-done.2
  64.5 0.0 copy-done.3
  64.5 0.0 copy-done.4
  64.5 4.1 %shard_map.120 = (bf16[128,4224]{1,0:T(8,128)(2,1)}, bf16[4,32,1152]{2,1,0:T(8,128)(2,1)S(1)}, bf16[4,32,1152]{2,1,0:T(8,128)(2,1)S(1)}, bf16[4,32,1152]{2,1,0:T...) custom-call(bf16[128,8320]{1,0:T(8,128)(2,1)S(1)} %bitcast.17, ...), custom_call_target="tpu_custom_call" | custom-call | flops 3221225472 | bytes 7929856 | tf_op jit(solution)/shard_map/pallas_call | solution.py:202
  68.6 4.8 %all-to-all-start.1 = ((bf16[16,8,4224]{2,1,0:T(8,128)(2,1)}), bf16[16,8,4224]{2,1,0:T(8,128)(2,1)S(1)}, u32[]{:S(2)}, u32[]{:S(2)}) async-start(bf16[16,8,4224]{2,1,0:T(8,128)(2,1)} %bitcast.8), calls=%async_computation.1 | async-start | bytes 2162688 | tf_op jit(solution)/shard_map/all_to_all | solution.py:275
  73.4 0.0 copy-start
  73.4 0.0 copy-start.1
  73.4 4.9 %collective-permute-start = (bf16[4,32,1152]{2,1,0:T(8,128)(2,1)S(1)}, bf16[4,32,1152]{2,1,0:T(8,128)(2,1)S(1)}, u32[]{:S(2)}, u32[]{:S(2)}) collective-permute-start(bf16[4,32,1152]{2,1,0:T(8,128)(2,1)S(1)} %get-tuple-element.22), channel_id=1, source_target_pairs={{0,96},{16,112},{32,64},{48,80},{64,32},{80,48},{96,0},{112,16},{1... | collective-permute-start | bytes 884744 | tf_op jit(solution)/shard_map/ppermute | solution.py:273
  78.4 2.4 %collective-permute-start.1 = (bf16[4,32,1152]{2,1,0:T(8,128)(2,1)S(1)}, bf16[4,32,1152]{2,1,0:T(8,128)(2,1)S(1)}, u32[]{:S(2)}, u32[]{:S(2)}) collective-permute-start(bf16[4,32,1152]{2,1,0:T(8,128)(2,1)S(1)} %get-tuple-element.23), channel_id=1, source_target_pairs={{0,32},{16,48},{32,0},{48,16},{64,96},{80,112},{96,64},{112,80},{1... | collective-permute-start | bytes 884744 | tf_op jit(solution)/shard_map/ppermute | solution.py:273
  80.8 3.4 %collective-permute-start.2 = (bf16[4,32,1152]{2,1,0:T(8,128)(2,1)S(1)}, bf16[4,32,1152]{2,1,0:T(8,128)(2,1)S(1)}, u32[]{:S(2)}, u32[]{:S(2)}) collective-permute-start(bf16[4,32,1152]{2,1,0:T(8,128)(2,1)S(1)} %get-tuple-element.24), channel_id=1, source_target_pairs={{0,64},{16,80},{32,96},{48,112},{64,0},{80,16},{96,32},{112,48},{1... | collective-permute-start | bytes 884744 | tf_op jit(solution)/shard_map/ppermute | solution.py:273
  84.2 3.2 %collective-permute-start.3 = (bf16[4,32,1152]{2,1,0:T(8,128)(2,1)S(1)}, bf16[4,32,1152]{2,1,0:T(8,128)(2,1)S(1)}, u32[]{:S(2)}, u32[]{:S(2)}) collective-permute-start(bf16[4,32,1152]{2,1,0:T(8,128)(2,1)S(1)} %get-tuple-element.25), channel_id=1, source_target_pairs={{0,48},{16,32},{32,16},{48,0},{64,112},{80,96},{96,80},{112,64},{1... | collective-permute-start | bytes 884744 | tf_op jit(solution)/shard_map/ppermute | solution.py:273
  87.4 3.6 %collective-permute-start.4 = (bf16[4,32,1152]{2,1,0:T(8,128)(2,1)S(1)}, bf16[4,32,1152]{2,1,0:T(8,128)(2,1)S(1)}, u32[]{:S(2)}, u32[]{:S(2)}) collective-permute-start(bf16[4,32,1152]{2,1,0:T(8,128)(2,1)S(1)} %get-tuple-element.26), channel_id=1, source_target_pairs={{0,80},{16,64},{32,112},{48,96},{64,16},{80,0},{96,48},{112,32},{1... | collective-permute-start | bytes 884744 | tf_op jit(solution)/shard_map/ppermute | solution.py:273
  91.0 0.0 collective-permute-done.refs_1_
  91.0 3.7 %collective-permute-start.5 = (bf16[4,32,1152]{2,1,0:T(8,128)(2,1)S(1)}, bf16[4,32,1152]{2,1,0:T(8,128)(2,1)S(1)}, u32[]{:S(2)}, u32[]{:S(2)}) collective-permute-start(bf16[4,32,1152]{2,1,0:T(8,128)(2,1)S(1)} %get-tuple-element.27), channel_id=1, source_target_pairs={{0,16},{16,0},{32,48},{48,32},{64,80},{80,64},{96,112},{112,96},{1... | collective-permute-start | bytes 884744 | tf_op jit(solution)/shard_map/ppermute | solution.py:273
  94.7 0.0 collective-permute-done.1.refs_2_
  94.7 3.3 %collective-permute-start.6 = (bf16[4,32,1152]{2,1,0:T(8,128)(2,1)S(1)}, bf16[4,32,1152]{2,1,0:T(8,128)(2,1)S(1)}, u32[]{:S(2)}, u32[]{:S(2)}) collective-permute-start(bf16[4,32,1152]{2,1,0:T(8,128)(2,1)S(1)} %get-tuple-element.28), channel_id=1, source_target_pairs={{0,112},{16,96},{32,80},{48,64},{64,48},{80,32},{96,16},{112,0},{1... | collective-permute-start | bytes 884744 | tf_op jit(solution)/shard_map/ppermute | solution.py:273
  98.0 0.0 collective-permute-done.2.refs_3_
  98.0 1.4 %collective-permute-done.3.refs_4_ = bf16[4,32,1152]{2,1,0:T(8,128)(2,1)S(1)} collective-permute-done((bf16[4,32,1152]{2,1,0:T(8,128)(2,1)S(1)}, bf16[4,32,1152]{2,1,0:T(8,128)(2,1)S(1)}, u32[]{:S(2)}, u32[]{:S(2)}) %collective-permute-start.3) | collective-permute-done | bytes 294944 | tf_op jit(solution)/shard_map/ppermute | solution.py:273
  99.4 0.0 collective-permute-done.4.refs_5_
  99.4 5.3 %collective-permute-done.5.refs_6_ = bf16[4,32,1152]{2,1,0:T(8,128)(2,1)S(1)} collective-permute-done((bf16[4,32,1152]{2,1,0:T(8,128)(2,1)S(1)}, bf16[4,32,1152]{2,1,0:T(8,128)(2,1)S(1)}, u32[]{:S(2)}, u32[]{:S(2)}) %collective-permute-start.5) | collective-permute-done | bytes 294944 | tf_op jit(solution)/shard_map/ppermute | solution.py:273
  104.7 1.4 %collective-permute-done.6.refs_7_ = bf16[4,32,1152]{2,1,0:T(8,128)(2,1)S(1)} collective-permute-done((bf16[4,32,1152]{2,1,0:T(8,128)(2,1)S(1)}, bf16[4,32,1152]{2,1,0:T(8,128)(2,1)S(1)}, u32[]{:S(2)}, u32[]{:S(2)}) %collective-permute-start.6) | collective-permute-done | bytes 294944 | tf_op jit(solution)/shard_map/ppermute | solution.py:273
  106.1 1.0 shard_map.121
  107.1 0.0 all-to-all-done.1
  107.1 9.4 %all-to-all-start.2 = ((bf16[4,32,1152]{2,1,0:T(8,128)(2,1)}), bf16[4,32,1152]{2,1,0:T(8,128)(2,1)S(1)}, u32[]{:S(2)}, u32[]{:S(2)}) async-start(bf16[4,32,1152]{2,1,0:T(8,128)(2,1)} %shard_map.121), calls=%async_computation.2 | async-start | bytes 589824 | tf_op jit(solution)/shard_map/all_to_all | solution.py:286
  116.5 0.0 copy-done
  116.5 0.0 copy-done.1
  116.5 2.0 %shard_map.122 = (bf16[256,1024]{1,0:T(8,128)(2,1)}, bf16[8,256]{1,0:T(8,128)(2,1)}) custom-call(bf16[128,4224]{1,0:T(8,128)(2,1)S(1)} %bitcast.16, s32[8,256]{1,0:T(8,128)S(1)} %bitcast.19, s32[8,256]{1,0:T(8,128)S(1)} %bitcast.21), custom_call_target="tpu_custom_call" | custom-call | flops 268435456 | bytes 1626112 | tf_op jit(solution)/shard_map/pallas_call | solution.py:202
  118.5 8.9 %all-to-all-done.2.parts_ref = bf16[4,32,1152]{2,1,0:T(8,128)(2,1)S(1)} async-done(((bf16[4,32,1152]{2,1,0:T(8,128)(2,1)}), bf16[4,32,1152]{2,1,0:T(8,128)(2,1)S(1)}, u32[]{:S(2)}, u32[]{:S(2)}) %all-to-all-start.2) | async-done | bytes 294944 | tf_op jit(solution)/shard_map/all_to_all | solution.py:286
  127.4 0.7 shard_map.123
Async XLA Ops:
  3.7 60.7 %copy-start.2 = (bf16[1,1024,384]{2,1,0:T(8,128)(2,1)S(1)}, bf16[1,1024,384]{2,1,0:T(8,128)(2,1)}, u32[]{:S(2)}) copy-start(bf16[1,1024,384]{2,1,0:T(8,128)(2,1)} %param.13) | copy-start | bytes 2359300
  3.8 60.7 %copy-start.3 = (bf16[1,1024,384]{2,1,0:T(8,128)(2,1)S(1)}, bf16[1,1024,384]{2,1,0:T(8,128)(2,1)}, u32[]{:S(2)}) copy-start(bf16[1,1024,384]{2,1,0:T(8,128)(2,1)} %param.14) | copy-start | bytes 2359300
  3.8 60.7 %copy-start.4 = (bf16[1,384,1024]{2,1,0:T(8,128)(2,1)S(1)}, bf16[1,384,1024]{2,1,0:T(8,128)(2,1)}, u32[]{:S(2)}) copy-start(bf16[1,384,1024]{2,1,0:T(8,128)(2,1)} %param.15) | copy-start | bytes 2359300
  68.6 38.5 %all-to-all-start.1 = ((bf16[16,8,4224]{2,1,0:T(8,128)(2,1)}), bf16[16,8,4224]{2,1,0:T(8,128)(2,1)S(1)}, u32[]{:S(2)}, u32[]{:S(2)}) async-start(bf16[16,8,4224]{2,1,0:T(8,128)(2,1)} %bitcast.8), calls=%async_computation.1 | async-start | bytes 2162688 | tf_op jit(solution)/shard_map/all_to_all | solution.py:275
  73.4 43.1 %copy-start = (s32[256,8]{0,1:T(8,128)S(1)}, s32[256,8]{0,1:T(8,128)}, u32[]{:S(2)}) copy-start(s32[256,8]{0,1:T(8,128)} %param.11) | copy-start | bytes 24580
  73.4 43.1 %copy-start.1 = (s32[256,8]{0,1:T(8,128)S(1)}, s32[256,8]{0,1:T(8,128)}, u32[]{:S(2)}) copy-start(s32[256,8]{0,1:T(8,128)} %param.12) | copy-start | bytes 24580
  73.4 17.6 %collective-permute-start = (bf16[4,32,1152]{2,1,0:T(8,128)(2,1)S(1)}, bf16[4,32,1152]{2,1,0:T(8,128)(2,1)S(1)}, u32[]{:S(2)}, u32[]{:S(2)}) collective-permute-start(bf16[4,32,1152]{2,1,0:T(8,128)(2,1)S(1)} %get-tuple-element.22), channel_id=1, source_target_pairs={{0,96},{16,112},{32,64},{48,80},{64,32},{80,48},{96,0},{112,16},{1... | collective-permute-start | bytes 884744 | tf_op jit(solution)/shard_map/ppermute | solution.py:273
  78.4 16.3 %collective-permute-start.1 = (bf16[4,32,1152]{2,1,0:T(8,128)(2,1)S(1)}, bf16[4,32,1152]{2,1,0:T(8,128)(2,1)S(1)}, u32[]{:S(2)}, u32[]{:S(2)}) collective-permute-start(bf16[4,32,1152]{2,1,0:T(8,128)(2,1)S(1)} %get-tuple-element.23), channel_id=1, source_target_pairs={{0,32},{16,48},{32,0},{48,16},{64,96},{80,112},{96,64},{112,80},{1... | collective-permute-start | bytes 884744 | tf_op jit(solution)/shard_map/ppermute | solution.py:273
  80.8 17.2 %collective-permute-start.2 = (bf16[4,32,1152]{2,1,0:T(8,128)(2,1)S(1)}, bf16[4,32,1152]{2,1,0:T(8,128)(2,1)S(1)}, u32[]{:S(2)}, u32[]{:S(2)}) collective-permute-start(bf16[4,32,1152]{2,1,0:T(8,128)(2,1)S(1)} %get-tuple-element.24), channel_id=1, source_target_pairs={{0,64},{16,80},{32,96},{48,112},{64,0},{80,16},{96,32},{112,48},{1... | collective-permute-start | bytes 884744 | tf_op jit(solution)/shard_map/ppermute | solution.py:273
  84.2 15.3 %collective-permute-start.3 = (bf16[4,32,1152]{2,1,0:T(8,128)(2,1)S(1)}, bf16[4,32,1152]{2,1,0:T(8,128)(2,1)S(1)}, u32[]{:S(2)}, u32[]{:S(2)}) collective-permute-start(bf16[4,32,1152]{2,1,0:T(8,128)(2,1)S(1)} %get-tuple-element.25), channel_id=1, source_target_pairs={{0,48},{16,32},{32,16},{48,0},{64,112},{80,96},{96,80},{112,64},{1... | collective-permute-start | bytes 884744 | tf_op jit(solution)/shard_map/ppermute | solution.py:273
  87.4 12.1 %collective-permute-start.4 = (bf16[4,32,1152]{2,1,0:T(8,128)(2,1)S(1)}, bf16[4,32,1152]{2,1,0:T(8,128)(2,1)S(1)}, u32[]{:S(2)}, u32[]{:S(2)}) collective-permute-start(bf16[4,32,1152]{2,1,0:T(8,128)(2,1)S(1)} %get-tuple-element.26), channel_id=1, source_target_pairs={{0,80},{16,64},{32,112},{48,96},{64,16},{80,0},{96,48},{112,32},{1... | collective-permute-start | bytes 884744 | tf_op jit(solution)/shard_map/ppermute | solution.py:273
  91.0 13.7 %collective-permute-start.5 = (bf16[4,32,1152]{2,1,0:T(8,128)(2,1)S(1)}, bf16[4,32,1152]{2,1,0:T(8,128)(2,1)S(1)}, u32[]{:S(2)}, u32[]{:S(2)}) collective-permute-start(bf16[4,32,1152]{2,1,0:T(8,128)(2,1)S(1)} %get-tuple-element.27), channel_id=1, source_target_pairs={{0,16},{16,0},{32,48},{48,32},{64,80},{80,64},{96,112},{112,96},{1... | collective-permute-start | bytes 884744 | tf_op jit(solution)/shard_map/ppermute | solution.py:273
  94.7 11.4 %collective-permute-start.6 = (bf16[4,32,1152]{2,1,0:T(8,128)(2,1)S(1)}, bf16[4,32,1152]{2,1,0:T(8,128)(2,1)S(1)}, u32[]{:S(2)}, u32[]{:S(2)}) collective-permute-start(bf16[4,32,1152]{2,1,0:T(8,128)(2,1)S(1)} %get-tuple-element.28), channel_id=1, source_target_pairs={{0,112},{16,96},{32,80},{48,64},{64,48},{80,32},{96,16},{112,0},{1... | collective-permute-start | bytes 884744 | tf_op jit(solution)/shard_map/ppermute | solution.py:273
  107.1 20.3 %all-to-all-start.2 = ((bf16[4,32,1152]{2,1,0:T(8,128)(2,1)}), bf16[4,32,1152]{2,1,0:T(8,128)(2,1)S(1)}, u32[]{:S(2)}, u32[]{:S(2)}) async-start(bf16[4,32,1152]{2,1,0:T(8,128)(2,1)} %shard_map.121), calls=%async_computation.2 | async-start | bytes 589824 | tf_op jit(solution)/shard_map/all_to_all | solution.py:286
